TPU v7x, 128 devices: a whole 4x4x4 slice. The times are simulated.
128 devices in a mesh: ctx: 16 (over x, z), tp: 8 (over y, core).
Axes of the slice: x: 4, y: 4, z: 4, core: 2. Of those that a mesh axis runs over, the one named last changes fastest.
Arguments:
- queries: bfloat16 [8192, 8192], P('ctx', 'tp'), may hold values from -5 to 5
- keys: bfloat16 [8192, 1024], P('ctx', 'tp'), may hold values from -5 to 5
- values: bfloat16 [8192, 1024], P('ctx', 'tp'), may hold values from -6 to 6
- outputs: bfloat16 [8192, 8192], P('ctx', 'tp'), may hold values from -2 to 2
- out_grad: bfloat16 [8192, 8192], P('ctx', 'tp'), may hold values from -6 to 6
- lengths: int32 [8], replicated, may hold values from 1 to 4608, 8192 in all
- w_query: bfloat16 [5120, 8192], P(None, 'tp'), may hold values from -0.078125 to 0.078125
- w_key: bfloat16 [5120, 1024], P(None, 'tp'), may hold values from -0.078125 to 0.078125
- w_value: bfloat16 [5120, 1024], P(None, 'tp'), may hold values from -0.078125 to 0.078125
Outputs:
- input_grad: bfloat16 [8192, 5120], P('ctx', 'tp')
All inputs are finite; a program needn't handle non-finite values.
Results may differ from a plain program's by a relative error of at most 0.02.
Values may be sent and summed in bfloat16 or wider, within the bound.
A program may use at most 128 MiB of HBM per device.

v0:
```python
import jax
import jax.numpy as jnp
from jax import lax
from jax.sharding import PartitionSpec as P

HD = 128


def shards(queries, keys, values, outputs, out_grad, lengths, w_query, w_key, w_value):
    row_count = queries.shape[0]
    half_rows = row_count // 2
    kv_local = keys.shape[1] // HD
    group_size = queries.shape[1] // HD // kv_local
    score_scale = HD ** (-0.5)
    devices = lax.axis_size("ctx")
    my_index = lax.axis_index("ctx")
    total_rows = row_count * devices
    doc_ends = jnp.cumsum(lengths, dtype=jnp.int32)
    positions = jnp.arange(total_rows, dtype=jnp.int32)
    doc_of = jnp.sum(
        (positions[:, None] >= doc_ends[None, :]).astype(jnp.int32), axis=1, dtype=jnp.int32
    )
    work_query, work_output, work_grad = (queries, outputs, out_grad)
    block_starts = [my_index * row_count, my_index * row_count + half_rows]
    shape_four = (row_count, kv_local, group_size, HD)
    query_four = work_query.reshape(shape_four)
    grad_four = work_grad.reshape(shape_four)
    row_delta = jnp.sum(
        grad_four.astype(jnp.float32) * work_output.reshape(shape_four).astype(jnp.float32), axis=3
    )
    row_delta = row_delta.transpose(1, 2, 0)
    query_blocks = [query_four[:half_rows], query_four[half_rows:]]
    grad_blocks = [grad_four[:half_rows], grad_four[half_rows:]]
    delta_blocks = [row_delta[:, :, :half_rows], row_delta[:, :, half_rows:]]

    def allowed_for(block_index, key_start):
        query_pos = block_starts[block_index] + jnp.arange(half_rows, dtype=jnp.int32)
        key_pos = key_start + jnp.arange(row_count, dtype=jnp.int32)
        query_doc = lax.dynamic_slice_in_dim(doc_of, block_starts[block_index], half_rows)
        key_doc = lax.dynamic_slice_in_dim(doc_of, key_start, row_count)
        return (key_pos[None, :] <= query_pos[:, None]) & (key_doc[None, :] == query_doc[:, None])

    def reaches(block_index, key_start):
        first_row = block_starts[block_index]
        last_row = first_row + half_rows - 1
        return (
            (key_start <= last_row)
            & (doc_of[key_start + row_count - 1] >= doc_of[first_row])
            & (doc_of[key_start] <= doc_of[last_row])
        )

    def block_scores(block_index, key_block):
        return (
            jnp.einsum(
                "qcgd,kcd->cgqk",
                query_blocks[block_index],
                key_block,
                preferred_element_type=jnp.float32,
            )
            * score_scale
        )

    def unchanged(block_state):
        return block_state

    def stats_step(running, current, key_start):
        key_block = current[0].reshape(row_count, kv_local, HD)
        updated = []
        for block_index in range(2):

            def stats_compute_block(block_state, block_index=block_index):
                row_top, weight_sum = block_state
                allowed = allowed_for(block_index, key_start)
                scores = jnp.where(allowed, block_scores(block_index, key_block), -1e30)
                new_top = jnp.maximum(row_top, jnp.max(scores, axis=3))
                weights = jnp.where(allowed, jnp.exp(scores - new_top[..., None]), 0.0)
                return (new_top, weight_sum * jnp.exp(row_top - new_top) + jnp.sum(weights, axis=3))

            updated.append(
                lax.cond(
                    reaches(block_index, key_start),
                    stats_compute_block,
                    unchanged,
                    running[block_index],
                )
            )
        return tuple(updated)

    def grad_step(query_grads, current, key_start, running):
        key_block = current[0].reshape(row_count, kv_local, HD)
        value_block = current[1].reshape(row_count, kv_local, HD)
        key_grad = jnp.zeros((row_count, kv_local, HD), jnp.float32)
        value_grad = jnp.zeros((row_count, kv_local, HD), jnp.float32)
        new_grads = []
        for block_index in range(2):

            def grad_compute_block(block_state, block_index=block_index):
                query_grad, key_part, value_part = block_state
                row_top, weight_sum = running[block_index]
                allowed = allowed_for(block_index, key_start)
                scores = jnp.where(allowed, block_scores(block_index, key_block), -1e30)
                probability = (
                    jnp.where(allowed, jnp.exp(scores - row_top[..., None]), 0.0)
                    / weight_sum[..., None]
                )
                prob_grad = jnp.einsum(
                    "qcgd,kcd->cgqk",
                    grad_blocks[block_index],
                    value_block,
                    preferred_element_type=jnp.float32,
                )
                score_grad = (
                    probability * (prob_grad - delta_blocks[block_index][..., None])
                ).astype(jnp.bfloat16)
                prob_low = probability.astype(jnp.bfloat16)
                query_grad = query_grad + jnp.einsum(
                    "cgqk,kcd->qcgd", score_grad, key_block, preferred_element_type=jnp.float32
                )
                key_part = key_part + jnp.einsum(
                    "cgqk,qcgd->kcd",
                    score_grad,
                    query_blocks[block_index],
                    preferred_element_type=jnp.float32,
                )
                value_part = value_part + jnp.einsum(
                    "cgqk,qcgd->kcd",
                    prob_low,
                    grad_blocks[block_index],
                    preferred_element_type=jnp.float32,
                )
                return (query_grad, key_part, value_part)

            result = lax.cond(
                reaches(block_index, key_start),
                grad_compute_block,
                unchanged,
                (query_grads[block_index], key_grad, value_grad),
            )
            new_grads.append(result[0])
            key_grad, value_grad = (result[1], result[2])
        return (tuple(new_grads), key_grad, value_grad)

    key_value = jnp.stack([keys, values])
    stats_shape = (kv_local, group_size, half_rows)
    running_start = tuple(
        (
            (jnp.full(stats_shape, -1e30, jnp.float32), jnp.zeros(stats_shape, jnp.float32))
            for block_index in range(2)
        )
    )
    grads_start = tuple(
        (jnp.zeros((half_rows, kv_local, group_size, HD), jnp.float32) for block_index in range(2))
    )

    def stacked(key_grad, value_grad):
        return jnp.stack(
            [
                key_grad.reshape(row_count, kv_local * HD),
                value_grad.reshape(row_count, kv_local * HD),
            ]
        )

    collected = lax.all_gather(key_value, "ctx", axis=1, tiled=True)

    def slice_of(turn_index):
        return lax.dynamic_slice_in_dim(collected, turn_index * row_count, row_count, 1)

    def stats_turn(turn_index, running):
        return stats_step(running, slice_of(turn_index), turn_index * row_count)

    running = lax.fori_loop(0, devices, stats_turn, running_start)

    def grad_turn(query_grads, turn_index):
        query_grads, key_grad, value_grad = grad_step(
            query_grads, slice_of(turn_index), turn_index * row_count, running
        )
        return (query_grads, stacked(key_grad, value_grad))

    query_grads, partials = lax.scan(grad_turn, grads_start, jnp.arange(devices, dtype=jnp.int32))
    key_grads = lax.psum_scatter(
        partials.astype(jnp.bfloat16), "ctx", scatter_dimension=0, tiled=True
    ).astype(jnp.float32)[0]
    query_grad = (
        (jnp.concatenate(query_grads, axis=0) * score_scale)
        .reshape(row_count, -1)
        .astype(jnp.bfloat16)
    )
    key_low = (key_grads[0] * score_scale).astype(jnp.bfloat16)
    value_low = key_grads[1].astype(jnp.bfloat16)
    contract = (((1,), (1,)), ((), ()))
    partial_sum = lax.dot_general(query_grad, w_query, contract, preferred_element_type=jnp.float32)
    partial_sum = partial_sum + lax.dot_general(
        key_low, w_key, contract, preferred_element_type=jnp.float32
    )
    partial_sum = partial_sum + lax.dot_general(
        value_low, w_value, contract, preferred_element_type=jnp.float32
    )
    return lax.psum_scatter(partial_sum.astype(jnp.bfloat16), "tp", scatter_dimension=1, tiled=True)


def solution(mesh):
    in_specs = (
        P("ctx", "tp"),
        P("ctx", "tp"),
        P("ctx", "tp"),
        P("ctx", "tp"),
        P("ctx", "tp"),
        P(),
        P(None, "tp"),
        P(None, "tp"),
        P(None, "tp"),
    )
    out_specs = P("ctx", "tp")
    return jax.shard_map(shards, mesh=mesh, in_specs=in_specs, out_specs=out_specs, check_vma=False)
```

profile of v0, /device:TPU:0, one launch (start us, length us, event | category | flops | bytes accessed | tf_op | source)
XLA Modules:
  0.0 815.7 jit_solution(8929376916009239285)
XLA Ops:
  6.5 1.9 pad_maximum_fusion
  9.3 2.1 fusion.102
  11.9 2.1 copy.62
  17.8 2.0 copy.64
  21.2 2.0 multiply_bitcast_fusion
  23.2 1.8 copy.66
  25.0 2.9 reduce_sum.43
  34.1 29.7 %all-gather.2.cloned.1.call-done = bf16[2,8192,128]{2,1,0:T(8,128)(2,1)} async-done(((bf16[2,512,128]{2,1,0:T(8,128)(2,1)}), bf16[2,8192,128]{2,1,0:T(8,128)(2,1)}) %all-gather.2.cloned.1.call-update) | async-done | bytes 4194320 | tf_op jit(solution)/shard_map/all_gather | solution.py:163
  65.0 123.5 %while.46 = (s32[]{:T(128)}, f32[1,8,256]{2,1,0:T(8,128)S(1)}, f32[1,8,256]{2,1,0:T(8,128)}, f32[1,8,256]{2,1,0:T(8,128)S(1)}, f32[1,8,256]{2,1,0:T(8,128)}, /*i...) while((s32[]{:T(128)}, f32[1,8,256]{2,1,0:T(8,128)S(1)}, ...), condition=%wide.region_11.12_spmd, body=%wide.region_2.11_spmd.sunk | while | flops 554444288 | bytes 19512168 | solution.py:171
  72.1 4.2 conditional.8
  76.3 4.2 conditional.9
  191.1 229.2 %while.47 = (s32[]{:T(128)}, f32[256,1,8,128]{3,0,2,1:T(8,128)}, f32[256,1,8,128]{3,0,2,1:T(8,128)}, bf16[16,2,512,128]{3,2,1,0:T(8,128)(2,1)}, s32[16]{0:T(128)...) while((s32[]{:T(128)}, f32[256,1,8,128]{3,0,2,1:T(8,128)}, ...), condition=%wide.region_18.19_spmd, body=%wide.region_13.18_spmd.sunk | while | flops 2705196544 | bytes 68304008 | solution.py:179
  201.0 9.6 %conditional.10 = (f32[256,1,8,128]{3,0,2,1:T(8,128)}, f32[512,1,128]{2,0,1:T(8,128)}, f32[512,1,128]{2,0,1:T(8,128)}) conditional(s32[]{:T(128)} %convert_element_type.150, f32[256,1,8,128]{3,0,2,1:T(8,128)} %get-tuple-element.1920, (s32[]{:T(128)}, s32[]{:T(128)}, s32[8192]{0:T(1024)}, bf16[512,1,128]{2,0,1:T(8,128)(2,1)}, ...), branch_computations={%region_14.14_spmd, %region_15.15_spmd} | conditional | flops 1352270592 | bytes 33234140 | solution.py:133
  202.7 2.3 fusion.13
  210.5 11.5 %conditional.11 = (f32[256,1,8,128]{3,0,2,1:T(8,128)}, f32[1,512,128]{2,1,0:T(8,128)}, f32[1,512,128]{2,1,0:T(8,128)}) conditional(s32[]{:T(128)} %convert_element_type.151, (f32[256,1,8,128]{3,0,2,1:T(8,128)}, f32[512,1,128]{2,0,1:T(8,128)}, f32[512,1,128]{2,0,1:T(8,128)}) %tuple.184, (s32[]{:T(128)}, s32[]{:T(128)}, s32[8192]{0:T(1024)}, ...), branch_computations={%region_16.16_spmd, %region_17.17_spmd} | conditional | flops 1352401664 | bytes 33758428 | solution.py:133
  212.3 2.3 fusion.45
  214.6 2.4 fusion.74
  217.7 2.4 fusion.65
  222.1 1.8 fusion.113
  235.2 1.8 fusion.113
  261.3 1.8 fusion.113
  300.6 1.8 fusion.113
  326.8 1.8 fusion.113
  339.9 1.8 fusion.113
  418.5 1.8 fusion.113
  423.2 11.2 %fusion.86 = f32[512,5120]{1,0:T(8,128)} fusion(bf16[5120,1024]{1,0:T(8,128)(2,1)} %param.27, f32[256,1024]{0,1:T(8,128)S(1)} %bitcast.317, f32[256,1024]{0,1:T(8,128)} %bitcast.316), kind=kOutput, calls=%fused_computation.93 | convolution fusion | flops 5370281984 | bytes 23068672 | tf_op jit(solution)/shard_map/dot_general | solution.py:191
  434.4 312.9 %all-reduce.3.cloned.1.call-done = bf16[16,2,512,128]{3,2,1,0:T(8,128)(2,1)} async-done(((bf16[16,2,512,128]{3,2,1,0:T(8,128)(2,1)}), bf16[16,2,512,128]{3,2,1,0:T(8,128)(2,1)}) %all-reduce.3.cloned.1.call-update) | async-done | bytes 4194320
  747.3 3.2 fusion.90
  750.5 8.9 %add_convert_fusion = bf16[512,5120]{1,0:T(8,128)(2,1)} fusion(f32[512,5120]{1,0:T(8,128)} %fusion.86, f32[512,5120]{1,0:T(8,128)S(1)} %fusion.90, bf16[5120,128]{1,0:T(8,128)(2,1)S(1)} %copy-done.10, bf16[16,2,512,128]{3,2,1,0:T(8,128)(2,1)} %all-reduce.3.cloned.1.call-done, u32[]{:T(128)} %bitcast.124, u32[]{:T(128)S(6)} %convert.2), kind=kOutput, calls=%fused_computation.89 | convolution fusion | flops 678952960 | bytes 27656708 | tf_op jit(solution)/shard_map/dot_general | solution.py:195
  759.4 7.9 copy.60
  767.3 39.7 %reduce-scatter.4.cloned.1.call-done = bf16[640,512]{1,0:T(8,128)(2,1)} async-done(((bf16[5120,512]{1,0:T(8,128)(2,1)}), bf16[640,512]{1,0:T(8,128)(2,1)}) %reduce-scatter.4.cloned.1.call-update) | async-done | bytes 655376
  807.0 2.2 copy.61
  (281 shorter events, 203.1 us)
Async XLA Ops:
  6.5 740.8 %copy-start = (bf16[5120,128]{1,0:T(8,128)(2,1)S(1)}, bf16[5120,128]{1,0:T(8,128)(2,1)}, u32[]{:S(2)}) copy-start(bf16[5120,128]{1,0:T(8,128)(2,1)} %param.28) | copy-start | bytes 3932164
  6.5 8.7 %copy-start.9 = (bf16[512,1024]{1,0:T(8,128)(2,1)S(1)}, bf16[512,1024]{1,0:T(8,128)(2,1)}, u32[]{:S(2)}) copy-start(bf16[512,1024]{1,0:T(8,128)(2,1)} %param.25) | copy-start | bytes 3145732
  6.5 57.2 %all-gather.2.cloned.1.call-start = ((), (), s32[]{:S(2)}) async-start(), calls=%async_computation.1 | async-start | bytes 4456448 | tf_op jit(solution)/shard_map/all_gather | solution.py:163
  8.4 738.9 %all-reduce.3.cloned.1.call-start = ((), (), s32[]{:S(2)}) async-start(), calls=%async_computation.3 | async-start | bytes 8388608
  73.8 1.8 copy-start.15
  75.7 0.6 copy-start.16
  78.0 1.8 copy-start.13
  79.9 0.6 copy-start.14
  205.0 1.4 copy-start.12
  206.4 2.2 copy-start.4
  206.5 2.2 copy-start.7
  209.5 1.0 copy-start.5
  214.6 2.4 copy-start.11
  217.0 3.2 copy-start.1
  217.0 3.2 copy-start.8
  221.1 1.0 copy-start.2
  420.3 0.7 copy-start.17
  420.3 1.2 copy-start.6
  420.3 2.6 copy-start.3
  420.3 386.7 %reduce-scatter.4.cloned.1.call-start = ((), (), s32[]{:S(2)}) async-start(), calls=%async_computation.2 | async-start | bytes 5898240
  747.3 3.2 copy-start.10
Sparse Core Ops, SparseCore 0:
  9.6 54.1 all-gather.1
  420.4 326.8 all-reduce.2
  767.5 39.5 reduce-scatter.3
where the time goes:
time: 825 us; the launch traced here: 816 us
  waiting for transfers between devices  382 us (46%)
  local copies, waits for them, and re-layouts  171 us (21%)
  loops' own time  169 us (20%)
  matrix products  40.4 us (5%)
  other arithmetic  39.6 us (5%)
  between operations  13.2 us (2%)
    unnamed x5, waiting for transfers between devices  353 us
    another operation x1, loops' own time, shards(): lax.scan(grad_turn, grads_start, jnp.arange(devices, dtype=jnp.int32))  90.7 us
    another operation x1, loops' own time, shards(): running = lax.fori_loop(0, devices, stats_turn, running_start)  77.9 us
    dynamic_slice x32, local copies, waits for them, and re-layouts, reaches(): doc_of[key_start] <= doc_of[last_row]  43.6 us
    all_gather x1, waiting for transfers between devices, shards(): collected = lax.all_gather(key_value, 'ctx', axis=1, tiled=True)  29.7 us
    dynamic_update_slice x16, other arithmetic, shards(): lax.scan(grad_turn, grads_start, jnp.arange(devices, dtype=jnp.int32))  28.3 us
    squeeze x16, local copies, waits for them, and re-layouts, grad_step(): value_block = current[1].reshape(row_count, kv_local, HD)  26.6 us
    another operation x36, local copies, waits for them, and re-layouts  25.1 us
  transfers between devices with their start and end apart: 3, of which 3 were waited for; matrix products, arithmetic and copies ran while one was open for 5% of the time, Pallas kernels for 0%

commit v1 on v0

v1 whole, which is shorter than its diff:
```python
import functools
import jax, jax.numpy as jnp
from jax import lax
from jax.experimental import pallas as pl
from jax.experimental.pallas import tpu as pltpu
from jax.sharding import PartitionSpec as P

HD = 128
CHUNK = 128
TILE = 256
NEG = -1e30
SAFE = 60.0
LAST = (((1,), (1,)), ((), ()))


def attention_kernel(total, start_ref, lengths_ref, q_ref, do_ref, delta_ref, k_ref, v_ref,
                     dq_ref, dk_ref, dv_ref, e_ref, ds_ref, mt_ref, q_rows, do_rows, q_over, do_over, kt_ref, dqt_ref,
                     dk_acc, dv_acc, stat_ref):
    rows = q_rows.shape[0]
    heads = rows // CHUNK
    pair = 2 * CHUNK
    pairs = rows // pair
    chunks = q_ref.shape[0] // CHUNK
    tiles = total // TILE
    scale = HD ** -0.5
    to_log2 = scale * 1.4426950408889634

    dk_acc[...] = jnp.zeros_like(dk_acc)
    dv_acc[...] = jnp.zeros_like(dv_acc)

    def turn_keys(i, most):
        turned = k_ref[pl.ds(pl.multiple_of(i * TILE, TILE), TILE), :].T
        kt_ref[i] = turned
        wide = turned.astype(jnp.float32)
        return jnp.maximum(most, jnp.sum(wide * wide, axis=0, keepdims=True))

    key_most = jnp.max(lax.fori_loop(0, tiles, turn_keys, jnp.zeros((1, TILE), jnp.float32)))

    def one_chunk(j, _):
        first = start_ref[j]
        t0 = pl.multiple_of(j * CHUNK, CHUNK)
        query_most = jnp.zeros((CHUNK, 1), jnp.float32)
        for h in range(heads):
            part = q_ref[pl.ds(t0, CHUNK), h * HD:(h + 1) * HD]
            q_rows[h * CHUNK:(h + 1) * CHUNK, :] = part
            do_rows[h * CHUNK:(h + 1) * CHUNK, :] = do_ref[pl.ds(t0, CHUNK), h * HD:(h + 1) * HD]
            wide = part.astype(jnp.float32)
            query_most = jnp.maximum(query_most, jnp.sum(wide * wide, axis=1, keepdims=True))
        small = jnp.max(query_most) * key_most * (to_log2 * to_log2) <= SAFE * SAFE
        query_pos = first + lax.broadcasted_iota(jnp.int32, (1, pair), 1) % CHUNK
        row_start = jnp.zeros((1, pair), jnp.int32)
        low, high = jnp.int32(0), jnp.int32(0)
        begin = jnp.int32(0)
        for d in range(lengths_ref.shape[0]):
            row_start = jnp.where(query_pos >= begin, begin, row_start)
            low = jnp.where(first >= begin, begin, low)
            high = jnp.where(first + CHUNK - 1 >= begin, begin, high)
            begin = begin + lengths_ref[d]
        tile_low = low // TILE
        tile_end = (first + CHUNK - 1) // TILE + 1
        plain_low = jnp.minimum((high + TILE - 1) // TILE, tile_end)
        plain_end = jnp.maximum((first + 1) // TILE, plain_low)
        edge = plain_low - tile_low
        edges = edge + tile_end - plain_end

        def edge_tile(n):
            return jnp.where(n < edge, tile_low + n, plain_end + n - edge)

        def allowed_of(key0):
            key_pos = key0 + lax.broadcasted_iota(jnp.int32, (TILE, pair), 0)
            return (key_pos >= row_start) & (key_pos <= query_pos)

        def scores(key, p):
            return lax.dot_general(key, q_rows[p * pair:(p + 1) * pair, :], LAST,
                                   preferred_element_type=jnp.float32) * to_log2

        def weigh(i, sums, masked):
            key0 = pl.multiple_of(i * TILE, TILE)
            key = k_ref[pl.ds(key0, TILE), :]
            new = []
            for p in range(pairs):
                e = jnp.exp2(scores(key, p))
                if masked:
                    e = jnp.where(allowed_of(key0), e, 0.0)
                new.append(sums[p] + jnp.sum(e.reshape(TILE // 8, 8, pair), axis=0))
                e_ref[i - tile_low, :, p * pair:(p + 1) * pair] = e.astype(jnp.bfloat16)
            return tuple(new)

        @pl.when(small)
        def _():
            sums = tuple(jnp.zeros((8, pair), jnp.float32) for _ in range(pairs))
            sums = lax.fori_loop(0, edges, lambda n, s: weigh(edge_tile(n), s, True), sums)
            sums = lax.fori_loop(plain_low, plain_end, lambda i, s: weigh(i, s, False), sums)
            for p in range(pairs):
                stat_ref[:, p * pair:(p + 1) * pair] = 1.0 / jnp.sum(sums[p], axis=0, keepdims=True)

        @pl.when(jnp.logical_not(small))
        def _():
            def step(i, carry):
                tops, sums = carry
                key0 = pl.multiple_of(i * TILE, TILE)
                key = k_ref[pl.ds(key0, TILE), :]
                new_tops, new_sums = [], []
                for p in range(pairs):
                    s = jnp.where(allowed_of(key0), scores(key, p), NEG)
                    top = jnp.maximum(tops[p], jnp.max(s, axis=0, keepdims=True))
                    e = jnp.exp2(s - top)
                    new_sums.append(sums[p] * jnp.exp2(tops[p] - top) + jnp.sum(e, axis=0, keepdims=True))
                    new_tops.append(top)
                    e_ref[i - tile_low, :, p * pair:(p + 1) * pair] = e.astype(jnp.bfloat16)
                    mt_ref[i - tile_low, :, p * pair:(p + 1) * pair] = top
                return tuple(new_tops), tuple(new_sums)

            tops, sums = lax.fori_loop(tile_low, tile_end, step, (
                tuple(jnp.full((1, pair), NEG, jnp.float32) for _ in range(pairs)),
                tuple(jnp.zeros((1, pair), jnp.float32) for _ in range(pairs))))

            def settle(i, _):
                for p in range(pairs):
                    part = slice(p * pair, (p + 1) * pair)
                    factor = jnp.exp2(mt_ref[i - tile_low, :, part] - tops[p])
                    e_ref[i - tile_low, :, part] = (
                        e_ref[i - tile_low, :, part].astype(jnp.float32) * factor).astype(jnp.bfloat16)
                return 0

            lax.fori_loop(tile_low, tile_end, settle, 0)
            for p in range(pairs):
                stat_ref[:, p * pair:(p + 1) * pair] = 1.0 / sums[p]

        for h in range(heads):
            part = slice(h * CHUNK, (h + 1) * CHUNK)
            inverse = jnp.broadcast_to(stat_ref[:, part], (HD, CHUNK)).T
            q_over[part, :] = (q_rows[part, :].astype(jnp.float32) * inverse).astype(jnp.bfloat16)
            do_over[part, :] = (do_rows[part, :].astype(jnp.float32) * inverse).astype(jnp.bfloat16)
        delta = [jnp.concatenate([delta_ref[2 * p:2 * p + 1, pl.ds(t0, CHUNK)],
                                  delta_ref[2 * p + 1:2 * p + 2, pl.ds(t0, CHUNK)]], axis=1) for p in range(pairs)]
        dqt_ref[...] = jnp.zeros_like(dqt_ref)

        def grad_step(i, _):
            key0 = pl.multiple_of(i * TILE, TILE)
            slot = i - tile_low
            value = v_ref[pl.ds(key0, TILE), :]
            key_t = kt_ref[i]
            for p in range(pairs):
                part = slice(p * pair, (p + 1) * pair)
                dp = lax.dot_general(value, do_rows[part, :], LAST, preferred_element_type=jnp.float32)
                ds_ref[:, part] = (e_ref[slot, :, part].astype(jnp.float32) * (dp - delta[p])).astype(jnp.bfloat16)
            dv_acc[pl.ds(key0, TILE), :] += jnp.dot(e_ref[slot], do_over[...], preferred_element_type=jnp.float32)
            dk_acc[pl.ds(key0, TILE), :] += jnp.dot(ds_ref[...], q_over[...], preferred_element_type=jnp.float32)
            dqt_ref[...] += jnp.dot(key_t, ds_ref[...], preferred_element_type=jnp.float32)
            return 0

        lax.fori_loop(tile_low, tile_end, grad_step, 0)
        for h in range(heads):
            part = slice(h * CHUNK, (h + 1) * CHUNK)
            dq_ref[pl.ds(t0, CHUNK), h * HD:(h + 1) * HD] = (
                dqt_ref[:, part] * (stat_ref[:, part] * scale)).T.astype(jnp.bfloat16)
        return 0

    lax.fori_loop(0, chunks, one_chunk, 0)

    def write(i, _):
        at = pl.ds(pl.multiple_of(i * TILE, TILE), TILE)
        dk_ref[at, :] = (dk_acc[at, :] * scale).astype(jnp.bfloat16)
        dv_ref[at, :] = dv_acc[at, :].astype(jnp.bfloat16)
        return 0

    lax.fori_loop(0, tiles, write, 0)


def attention(starts, lengths, q, do, delta, k, v, longest=4608):
    total = k.shape[0]
    rows = q.shape[1] // HD * CHUNK
    max_tiles = (longest + CHUNK) // TILE + 2
    vmem = pl.BlockSpec(memory_space=pltpu.VMEM)
    smem = pl.BlockSpec(memory_space=pltpu.SMEM)
    return pl.pallas_call(
        functools.partial(attention_kernel, total),
        out_shape=[jax.ShapeDtypeStruct(q.shape, jnp.bfloat16),
                   jax.ShapeDtypeStruct(k.shape, jnp.bfloat16),
                   jax.ShapeDtypeStruct(k.shape, jnp.bfloat16)],
        in_specs=[smem, smem] + [vmem] * 5,
        out_specs=[vmem] * 3,
        scratch_shapes=[
            pltpu.VMEM((max_tiles, TILE, rows), jnp.bfloat16),
            pltpu.VMEM((TILE, rows), jnp.bfloat16),
            pltpu.VMEM((max_tiles, 1, rows), jnp.float32),
            pltpu.VMEM((rows, HD), jnp.bfloat16),
            pltpu.VMEM((rows, HD), jnp.bfloat16),
            pltpu.VMEM((rows, HD), jnp.bfloat16),
            pltpu.VMEM((rows, HD), jnp.bfloat16),
            pltpu.VMEM((total // TILE, HD, TILE), jnp.bfloat16),
            pltpu.VMEM((HD, rows), jnp.float32),
            pltpu.VMEM((total, HD), jnp.float32),
            pltpu.VMEM((total, HD), jnp.float32),
            pltpu.VMEM((1, rows), jnp.float32),
        ],
        compiler_params=pltpu.CompilerParams(vmem_limit_bytes=60 * 2**20),
        name="attention",
    )(starts, lengths, q, do, delta, k, v)


def shards(queries, keys, values, outputs, out_grad, lengths, w_query, w_key, w_value):
    row_count = queries.shape[0]
    heads = queries.shape[1] // HD
    me = lax.axis_index("ctx")
    starts = me * row_count + jnp.arange(row_count // CHUNK, dtype=jnp.int32) * CHUNK
    delta = jnp.sum(
        (out_grad.astype(jnp.float32) * outputs.astype(jnp.float32)).reshape(row_count, heads, HD), axis=2
    ).T
    collected = lax.all_gather(jnp.stack([keys, values]), "ctx", axis=1, tiled=True)
    query_grad, key_terms, value_terms = attention(
        starts, lengths, queries, out_grad, delta, collected[0], collected[1]
    )
    devices = lax.axis_size("ctx")
    partials = jnp.stack(
        [key_terms.reshape(devices, row_count, HD), value_terms.reshape(devices, row_count, HD)], axis=1
    )
    summed = lax.psum_scatter(partials, "ctx", scatter_dimension=0, tiled=True)[0]
    contract = (((1,), (1,)), ((), ()))
    total = lax.dot_general(query_grad, w_query, contract, preferred_element_type=jnp.float32)
    total = total + lax.dot_general(summed[0], w_key, contract, preferred_element_type=jnp.float32)
    total = total + lax.dot_general(summed[1], w_value, contract, preferred_element_type=jnp.float32)
    return lax.psum_scatter(total.astype(jnp.bfloat16), "tp", scatter_dimension=1, tiled=True)


def solution(mesh):
    in_specs = (P("ctx", "tp"),) * 5 + (P(),) + (P(None, "tp"),) * 3
    return jax.shard_map(shards, mesh=mesh, in_specs=in_specs, out_specs=P("ctx", "tp"), check_vma=False)
```

time: 825 us -> 346 us (0.42); the launches traced: 816 us -> 346 us
  loops' own time: 169 us -> 0 us
  local copies, waits for them, and re-layouts: 171 us -> 18 us
  waiting for transfers between devices: 382 us -> 260 us
  other arithmetic: 39.6 us -> 10.2 us
  Pallas kernels: 0 us -> 19.6 us
  matrix products: 40.4 us -> 24.2 us
    another operation x66 -> x0, loops' own time: 169 us -> none  [the longest x1 90.7 us: shards(): lax.scan(grad_turn, grads_start, jnp.arange(devices, dtype=jnp.int32))]
    unnamed x5, waiting for transfers between devices: 353 us -> 211 us
    dynamic_slice x57 -> x0, local copies, waits for them, and re-layouts: 70.2 us -> none  [the longest x32 43.6 us: reaches(): doc_of[key_start] <= doc_of[last_row]]
    squeeze x32 -> x1, local copies, waits for them, and re-layouts: 41.3 us -> 4.48 us  [shards(): collected[1]]
    dynamic_update_slice x16 -> x0, other arithmetic: 28.3 us -> none  [shards(): lax.scan(grad_turn, grads_start, jnp.arange(devices, dtype=jnp.int32))]
    another operation x36 -> x0, local copies, waits for them, and re-layouts: 25.1 us -> none
    all_gather x1, waiting for transfers between devices: 29.7 us -> 49.4 us  [shards(): lax.all_gather(jnp.stack([keys, values]), 'ctx', axis=1, tiled=True)]
    pallas_call x0 -> x1, Pallas kernels: none -> 19.6 us  [attention(): pl.pallas_call(functools.partial(attention_kernel, total), out_shape=[jax...]
where the time goes in v1:
time: 346 us
  waiting for transfers between devices  260 us (75%)
  matrix products  24.2 us (7%)
  Pallas kernels  19.6 us (6%)
  local copies, waits for them, and re-layouts  18 us (5%)
  between operations  13.2 us (4%)
  other arithmetic  10.2 us (3%)
    unnamed x5, waiting for transfers between devices  211 us
    all_gather x1, waiting for transfers between devices, shards(): lax.all_gather(jnp.stack([keys, values]), 'ctx', axis=1, tiled=True)  49.4 us
    pallas_call x1, Pallas kernels, attention(): pl.pallas_call(functools.partial(attention_kernel, total), out_shape=[jax...  19.6 us
    dot_general x1, matrix products, shards(): lax.dot_general(query_grad, w_query, contract, preferred_element_type=jnp...  12.1 us
    unnamed x14, local copies, waits for them, and re-layouts  11.8 us
    dot_general x1, matrix products, shards(): lax.dot_general(summed[1], w_value, contract, preferred_element_type=jnp....  8.93 us
  transfers between devices with their start and end apart: 3, of which 3 were waited for; matrix products, arithmetic and copies ran while one was open for 5% of the time, Pallas kernels for 0%

profile of v1, /device:TPU:0, one launch (start us, length us, event | category | flops | bytes accessed | tf_op | source)
XLA Modules:
  0.0 345.7 jit_solution(6732414392980834471)
XLA Ops:
  6.5 0.0 copy-start
  6.5 0.0 all-gather.2.cloned.1.call-start
  6.5 1.8 pad_maximum_fusion.1
  8.3 0.0 all-gather.2.cloned.1.call-update
  8.4 0.0 all-reduce.3.cloned.1.call-start
  8.4 1.9 multiply_bitcast_fusion
  10.4 0.5 copy.15
  10.8 1.3 reduce_sum.9
  12.1 1.6 copy.10
  13.8 0.5 multiply_add_fusion.start_ref
  14.3 49.4 %all-gather.2.cloned.1.call-done = bf16[2,8192,128]{2,1,0:T(8,128)(2,1)} async-done(((bf16[2,512,128]{2,1,0:T(8,128)(2,1)}), bf16[2,8192,128]{2,1,0:T(8,128)(2,1)}) %all-gather.2.cloned.1.call-update) | async-done | bytes 4194320 | tf_op jit(solution)/shard_map/all_gather | solution.py:211
  63.8 4.5 %slice_bitcast_fusion = (bf16[8192,128]{1,0:T(8,128)(2,1)}, bf16[8192,128]{1,0:T(8,128)(2,1)}) fusion(bf16[2,8192,128]{2,1,0:T(8,128)(2,1)} %all-gather.2.cloned.1.call-done), kind=kLoop, calls=%fused_computation.2 | loop fusion | bytes 8388608 | tf_op jit(solution)/shard_map/squeeze | solution.py:213
  68.2 19.6 %attention.1 = (bf16[512,1024]{1,0:T(8,128)(2,1)}, bf16[8192,128]{1,0:T(8,128)(2,1)}, bf16[8192,128]{1,0:T(8,128)(2,1)}) custom-call(s32[4]{0:T(128)} %multiply_add_fusion.start_ref, s32[8]{0:T(128)} %lengths_ref.1, bf16[512,1024]{1,0:T(8,128)(2,1)} %q_ref.1, bf16[512,1024]{1,0:T(8,128)(2,1)} %do_ref.1, f32[8,512]{1,0:T(8,128)} %bitcast.38, ...), custom_call_target="tpu_custom_call" | custom-call | tf_op jit(solution)/shard_map/attention/pallas_call | solution.py:177
  87.8 4.7 %pad_maximum_fusion = bf16[16,2,512,128]{3,2,0,1:T(8,128)(2,1)} fusion(bf16[16,1,512,128]{3,2,0,1:T(8,128)(2,1)} %bitcast.34, bf16[16,1,512,128]{3,2,0,1:T(8,128)(2,1)} %bitcast.33), kind=kLoop, calls=%fused_computation.1 | loop fusion | flops 2097152 | bytes 8388608 | tf_op jit(solution)/shard_map/stack | solution.py:216
  92.5 0.0 copy-start.4
  92.5 0.0 copy-start.3
  92.5 0.0 all-reduce.3.cloned.1.call-update
  92.5 0.0 reduce-scatter.7.cloned.1.call-start
  92.6 0.6 copy-done.4
  93.1 0.6 dynamic-slice
  93.7 0.0 copy-done.3
  93.7 12.1 %fusion.3 = f32[512,5120]{1,0:T(8,128)} fusion(bf16[512,1024]{1,0:T(8,128)(2,1)S(1)} %copy-done.3, bf16[5120,1024]{1,0:T(8,128)(2,1)} %param.15), kind=kOutput, calls=%fused_computation.12 | convolution fusion | flops 5368709120 | bytes 22020096 | tf_op jit(solution)/shard_map/dot_general | solution.py:221
  105.9 171.3 %all-reduce.3.cloned.1.call-done = bf16[16,2,512,128]{3,2,0,1:T(8,128)(2,1)} async-done(((bf16[16,2,512,128]{3,2,0,1:T(8,128)(2,1)}), bf16[16,2,512,128]{3,2,0,1:T(8,128)(2,1)}) %all-reduce.3.cloned.1.call-update) | async-done | bytes 4194320
  277.1 0.0 copy-done
  277.1 3.2 fusion
  280.3 0.0 copy-done.2
  280.3 8.9 %add_convert_fusion = bf16[512,5120]{1,0:T(8,128)(2,1)} fusion(f32[512,5120]{1,0:T(8,128)} %fusion.3, f32[512,5120]{1,0:T(8,128)S(1)} %fusion, bf16[5120,128]{1,0:T(8,128)(2,1)S(1)} %copy-done.2, bf16[16,2,512,128]{3,2,0,1:T(8,128)(2,1)} %all-reduce.3.cloned.1.call-done, u32[]{:T(128)} %bitcast.17, u32[]{:T(128)S(6)} %convert), kind=kOutput, calls=%fused_computation | convolution fusion | flops 678952960 | bytes 27656708 | tf_op jit(solution)/shard_map/dot_general | solution.py:223
  289.3 8.0 %copy.13 = bf16[512,5120]{0,1:T(8,128)(2,1)} copy(bf16[512,5120]{1,0:T(8,128)(2,1)} %add_convert_fusion) | data formatting | bytes 10485760
  297.3 0.0 reduce-scatter.7.cloned.1.call-update
  297.3 39.7 %reduce-scatter.7.cloned.1.call-done = bf16[640,512]{1,0:T(8,128)(2,1)} async-done(((bf16[5120,512]{1,0:T(8,128)(2,1)}), bf16[640,512]{1,0:T(8,128)(2,1)}) %reduce-scatter.7.cloned.1.call-update) | async-done | bytes 655376
  337.0 2.2 copy.14
  339.2 0.0 copy-done.1
  (2 shorter events, 0.0 us)
Async XLA Ops:
  6.5 270.6 %copy-start = (bf16[5120,128]{1,0:T(8,128)(2,1)S(1)}, bf16[5120,128]{1,0:T(8,128)(2,1)}, u32[]{:S(2)}) copy-start(bf16[5120,128]{1,0:T(8,128)(2,1)} %param.16) | copy-start | bytes 3932164
  6.5 57.2 %all-gather.2.cloned.1.call-start = ((), (), s32[]{:S(2)}) async-start(), calls=%async_computation.1 | async-start | bytes 4456448 | tf_op jit(solution)/shard_map/all_gather | solution.py:211
  8.4 268.8 %all-reduce.3.cloned.1.call-start = ((), (), s32[]{:S(2)}) async-start(), calls=%async_computation.3 | async-start | bytes 8388608
  92.5 0.7 copy-start.4
  92.5 1.2 copy-start.3
  92.5 244.5 %reduce-scatter.7.cloned.1.call-start = ((), (), s32[]{:S(2)}) async-start(), calls=%async_computation.2 | async-start | bytes 5898240
  277.1 3.2 copy-start.2
  289.3 49.9 %copy-start.1 = (bf16[5120,128]{1,0:T(8,128)(2,1)S(1)}, bf16[5120,128]{1,0:T(8,128)(2,1)}, u32[]{:S(2)}) copy-start(bf16[5120,128]{1,0:T(8,128)(2,1)} %param.16) | copy-start | bytes 3932164
Sparse Core Ops, SparseCore 0:
  9.6 54.1 all-gather.1
  92.6 184.4 all-reduce.2
  297.4 39.5 reduce-scatter.6

commit v2 on v1

--- a/solution.py
+++ b/solution.py
@@ -13,8 +13,8 @@
 LAST = (((1,), (1,)), ((), ()))
 
 
-def attention_kernel(total, start_ref, lengths_ref, q_ref, do_ref, delta_ref, k_ref, v_ref,
-                     dq_ref, dk_ref, dv_ref, e_ref, ds_ref, mt_ref, q_rows, do_rows, q_over, do_over, kt_ref, dqt_ref,
+def attention_kernel(total, start_ref, lengths_ref, q_ref, do_ref, delta_ref, kv_ref,
+                     dq_ref, dkv_ref, e_ref, ds_ref, mt_ref, q_rows, do_rows, q_over, do_over, kt_ref, dqt_ref,
                      dk_acc, dv_acc, stat_ref):
     rows = q_rows.shape[0]
     heads = rows // CHUNK
@@ -29,7 +29,7 @@
     dv_acc[...] = jnp.zeros_like(dv_acc)
 
     def turn_keys(i, most):
-        turned = k_ref[pl.ds(pl.multiple_of(i * TILE, TILE), TILE), :].T
+        turned = kv_ref[pl.ds(pl.multiple_of(i * TILE, TILE), TILE), :HD].T
         kt_ref[i] = turned
         wide = turned.astype(jnp.float32)
         return jnp.maximum(most, jnp.sum(wide * wide, axis=0, keepdims=True))
@@ -76,7 +76,7 @@
 
         def weigh(i, sums, masked):
             key0 = pl.multiple_of(i * TILE, TILE)
-            key = k_ref[pl.ds(key0, TILE), :]
+            key = kv_ref[pl.ds(key0, TILE), :HD]
             new = []
             for p in range(pairs):
                 e = jnp.exp2(scores(key, p))
@@ -99,7 +99,7 @@
             def step(i, carry):
                 tops, sums = carry
                 key0 = pl.multiple_of(i * TILE, TILE)
-                key = k_ref[pl.ds(key0, TILE), :]
+                key = kv_ref[pl.ds(key0, TILE), :HD]
                 new_tops, new_sums = [], []
                 for p in range(pairs):
                     s = jnp.where(allowed_of(key0), scores(key, p), NEG)
@@ -139,7 +139,7 @@
         def grad_step(i, _):
             key0 = pl.multiple_of(i * TILE, TILE)
             slot = i - tile_low
-            value = v_ref[pl.ds(key0, TILE), :]
+            value = kv_ref[pl.ds(key0, TILE), HD:]
             key_t = kt_ref[i]
             for p in range(pairs):
                 part = slice(p * pair, (p + 1) * pair)
@@ -161,15 +161,15 @@
 
     def write(i, _):
         at = pl.ds(pl.multiple_of(i * TILE, TILE), TILE)
-        dk_ref[at, :] = (dk_acc[at, :] * scale).astype(jnp.bfloat16)
-        dv_ref[at, :] = dv_acc[at, :].astype(jnp.bfloat16)
+        dkv_ref[at, :HD] = (dk_acc[at, :] * scale).astype(jnp.bfloat16)
+        dkv_ref[at, HD:] = dv_acc[at, :].astype(jnp.bfloat16)
         return 0
 
     lax.fori_loop(0, tiles, write, 0)
 
 
-def attention(starts, lengths, q, do, delta, k, v, longest=4608):
-    total = k.shape[0]
+def attention(starts, lengths, q, do, delta, kv, longest=4608):
+    total = kv.shape[0]
     rows = q.shape[1] // HD * CHUNK
     max_tiles = (longest + CHUNK) // TILE + 2
     vmem = pl.BlockSpec(memory_space=pltpu.VMEM)
@@ -177,10 +177,9 @@
     return pl.pallas_call(
         functools.partial(attention_kernel, total),
         out_shape=[jax.ShapeDtypeStruct(q.shape, jnp.bfloat16),
-                   jax.ShapeDtypeStruct(k.shape, jnp.bfloat16),
-                   jax.ShapeDtypeStruct(k.shape, jnp.bfloat16)],
-        in_specs=[smem, smem] + [vmem] * 5,
-        out_specs=[vmem] * 3,
+                   jax.ShapeDtypeStruct(kv.shape, jnp.bfloat16)],
+        in_specs=[smem, smem] + [vmem] * 4,
+        out_specs=[vmem] * 2,
         scratch_shapes=[
             pltpu.VMEM((max_tiles, TILE, rows), jnp.bfloat16),
             pltpu.VMEM((TILE, rows), jnp.bfloat16),
@@ -197,31 +196,374 @@
         ],
         compiler_params=pltpu.CompilerParams(vmem_limit_bytes=60 * 2**20),
         name="attention",
-    )(starts, lengths, q, do, delta, k, v)
+    )(starts, lengths, q, do, delta, kv)
+
+
+SIDE = 4
+MESH = pl.DeviceIdType.MESH
+
+
+def ring_place(axis, step):
+    me = lax.axis_index("ctx")
+    x, z = me // SIDE, me % SIDE
+    if axis == 0:
+        return lax.rem(x + step + SIDE, SIDE) * SIDE + z
+    return x * SIDE + lax.rem(z + step + SIDE, SIDE)
+
+
+def block_at(axis, first, second):
+    me = lax.axis_index("ctx")
+    x, z = me // SIDE, me % SIDE
+    along, across = (first, second) if axis == 0 else (second, first)
+    return lax.rem(x + along + SIDE, SIDE) * SIDE + lax.rem(z + across + SIDE, SIDE)
+
+
+def greet(partners):
+    barrier = pltpu.get_barrier_semaphore()
+    for partner in partners:
+        pl.semaphore_signal(barrier, inc=1, device_id=partner, device_id_type=MESH)
+    pl.semaphore_wait(barrier, len(partners))
+
+
+def collect_kernel(k_ref, v_ref, out_grad_ref, outputs_ref, kv_ref, delta_ref, local_sem, send_sem, recv_sem):
+    me = lax.axis_index("ctx")
+    rows = k_ref.shape[0]
+    half = rows // 2
+    quarter = half // 2
+    own = [
+        pltpu.make_async_copy(k_ref, kv_ref.at[me, :, pl.ds(0, HD)], local_sem.at[0]),
+        pltpu.make_async_copy(v_ref, kv_ref.at[me, :, pl.ds(HD, HD)], local_sem.at[1]),
+    ]
+    for copy in own:
+        copy.start()
+    greet([{"ctx": ring_place(axis, step)} for axis in (0, 1) for step in (1, -1)])
+    for copy in own:
+        copy.wait()
+    copies = {}
+
+    def begin(name, number, axis, step, block, start, count):
+        region = kv_ref.at[block, pl.ds(start, count), :]
+        copy = pltpu.make_async_remote_copy(
+            src_ref=region, dst_ref=region, send_sem=send_sem.at[number], recv_sem=recv_sem.at[number],
+            device_id={"ctx": ring_place(axis, step)}, device_id_type=MESH)
+        copy.start()
+        copies[name] = copy
+
+    def near(h, item, shift):
+        axis = h if item == "line" else 1 - h
+        base = h * 20 + (0 if item == "line" else 4 + 4 * item)
+        block = me if item == "line" else block_at(h, shift, 0)
+        begin((h, item, 0), base, axis, 1, block, h * half, half)
+        begin((h, item, 1), base + 1, axis, -1, block, h * half, half)
+
+    def far(h, item, shift):
+        axis = h if item == "line" else 1 - h
+        base = h * 20 + (0 if item == "line" else 4 + 4 * item)
+
+        def block(step):
+            return block_at(h, step, 0) if item == "line" else block_at(h, shift, step)
+
+        copies[h, item, 0].wait_recv()
+        begin((h, item, 2), base + 2, axis, 1, block(-1), h * half, quarter)
+        copies[h, item, 1].wait_recv()
+        begin((h, item, 3), base + 3, axis, -1, block(1), h * half + quarter, quarter)
+
+    shifts = (0, -1, 1, 2)
+    for h in (0, 1):
+        near(h, "line", 0)
+    for h in (0, 1):
+        near(h, 0, shifts[0])
+    for head in range(delta_ref.shape[0]):
+        part = slice(head * HD, (head + 1) * HD)
+        product = out_grad_ref[:, part].astype(jnp.float32) * outputs_ref[:, part].astype(jnp.float32)
+        delta_ref[head:head + 1, :] = jnp.sum(product.T, axis=0, keepdims=True)
+    for h in (0, 1):
+        far(h, "line", 0)
+        near(h, 1, shifts[1])
+        near(h, 2, shifts[2])
+    for h in (0, 1):
+        far(h, 0, shifts[0])
+    for h in (0, 1):
+        copies[h, "line", 2].wait_recv()
+        copies[h, "line", 3].wait_recv()
+        near(h, 3, shifts[3])
+    for item in (1, 2, 3):
+        for h in (0, 1):
+            far(h, item, shifts[item])
+    for item in (0, 1, 2, 3):
+        for h in (0, 1):
+            copies[h, item, 2].wait_recv()
+            copies[h, item, 3].wait_recv()
+    for copy in copies.values():
+        copy.wait_send()
+
+
+def collect(keys, values, out_grad, outputs):
+    rows = keys.shape[0]
+    heads = out_grad.shape[1] // HD
+    vmem = pl.BlockSpec(memory_space=pltpu.VMEM)
+    anywhere = pl.BlockSpec(memory_space=pl.ANY)
+    return pl.pallas_call(
+        collect_kernel,
+        out_shape=[jax.ShapeDtypeStruct((SIDE * SIDE, rows, 2 * HD), jnp.bfloat16),
+                   jax.ShapeDtypeStruct((heads, rows), jnp.float32)],
+        in_specs=[anywhere, anywhere, vmem, vmem],
+        out_specs=[anywhere, vmem],
+        scratch_shapes=[pltpu.SemaphoreType.DMA((2,)), pltpu.SemaphoreType.DMA((40,)), pltpu.SemaphoreType.DMA((40,))],
+        compiler_params=pltpu.CompilerParams(collective_id=0, has_side_effects=True, vmem_limit_bytes=32 * 2**20),
+        name="collect",
+    )(keys, values, out_grad, outputs)
+
+
+PARTS = 2
+RS_ORDER = (2, -1, 1, 0)
+
+
+def tp_place(step, core):
+    y = lax.axis_index("tp") // 2
+    return lax.rem(y + step + SIDE, SIDE) * 2 + core
+
+
+def finish_kernel(dq_ref, dkv_hbm, wq_hbm, wk_hbm, wv_hbm, out_ref, dkv_ref, wq_ref, wkv_ref, acc_ref, sum_ref,
+                  low_ref, high_ref, stage_ref, fin_ref, res_ref, pair_out, pair_in, y_stage, y_low, y_high, y_fin,
+                  load_sem, send_sem, recv_sem):
+    core = lax.axis_index("tp") % 2
+    rows = dq_ref.shape[0]
+    half = rows // 2
+    size = half // PARTS
+    mid = size // 2
+    loads = [
+        pltpu.make_async_copy(dkv_hbm, dkv_ref, load_sem.at[0]),
+        pltpu.make_async_copy(wq_hbm, wq_ref, load_sem.at[1]),
+        pltpu.make_async_copy(wk_hbm, wkv_ref.at[:, :, pl.ds(0, HD)], load_sem.at[2]),
+        pltpu.make_async_copy(wv_hbm, wkv_ref.at[:, :, pl.ds(HD, HD)], load_sem.at[3]),
+    ]
+    for copy in loads:
+        copy.start()
+    greet([{"ctx": ring_place(axis, step)} for axis in (0, 1) for step in (1, -1)]
+          + [{"tp": tp_place(step, core)} for step in (1, -1)] + [{"tp": tp_place(0, 1 - core)}])
+    copies = {}
+
+    def begin(name, number, device, src, dst):
+        copy = pltpu.make_async_remote_copy(src_ref=src, dst_ref=dst, send_sem=send_sem.at[number],
+                                            recv_sem=recv_sem.at[number], device_id=device, device_id_type=MESH)
+        copy.start()
+        copies[name] = copy
+
+    def wide(value):
+        return value.astype(jnp.float32)
+
+    def ident(s, h, k):
+        return (s * 2 + h) * 5 + (4 if k is None else RS_ORDER.index(k))
+
+    def term(s, h, k, shift, start, count):
+        if k is None:
+            return res_ref.at[s, h, RS_ORDER.index(shift), pl.ds(start, count), :]
+        return dkv_ref.at[block_at(h, k, shift), pl.ds(h * half + s * size + start, count), :]
+
+    def ring_axis(h, k):
+        return h if k is None else 1 - h
+
+    def reduce_send(s, h, k):
+        n, axis = ident(s, h, k), ring_axis(h, k)
+        begin(("low", n), 4 * n, {"ctx": ring_place(axis, 1)}, term(s, h, k, 2, 0, mid), low_ref.at[n])
+        begin(("high", n), 4 * n + 1, {"ctx": ring_place(axis, -1)}, term(s, h, k, 2, mid, mid), high_ref.at[n])
+
+    def reduce_pass(s, h, k):
+        n, axis = ident(s, h, k), ring_axis(h, k)
+        copies["low", n].wait_recv()
+        stage_ref[n, 0, :mid, :] = (wide(term(s, h, k, 1, 0, mid)[...]) + wide(low_ref[n])).astype(jnp.bfloat16)
+        stage_ref[n, 0, mid:, :] = term(s, h, k, 1, mid, mid)[...]
+        begin(("up", n), 4 * n + 2, {"ctx": ring_place(axis, 1)}, stage_ref.at[n, 0], fin_ref.at[n, 0])
+        copies["high", n].wait_recv()
+        stage_ref[n, 1, :mid, :] = term(s, h, k, -1, 0, mid)[...]
+        stage_ref[n, 1, mid:, :] = (wide(term(s, h, k, -1, mid, mid)[...]) + wide(high_ref[n])).astype(jnp.bfloat16)
+        begin(("down", n), 4 * n + 3, {"ctx": ring_place(axis, -1)}, stage_ref.at[n, 1], fin_ref.at[n, 1])
+
+    def reduce_end(s, h, k):
+        n = ident(s, h, k)
+        copies["up", n].wait_recv()
+        copies["down", n].wait_recv()
+        total = wide(term(s, h, k, 0, 0, size)[...]) + wide(fin_ref[n, 0]) + wide(fin_ref[n, 1])
+        if k is None:
+            sum_ref[pl.ds(h * half + s * size, size), :] = total.astype(jnp.bfloat16)
+        else:
+            res_ref[s, h, RS_ORDER.index(k)] = total.astype(jnp.bfloat16)
+
+    def reduce_steps(s):
+        for k in RS_ORDER:
+            for h in (0, 1):
+                reduce_send(s, h, k)
+        yield
+        for k in RS_ORDER:
+            for h in (0, 1):
+                reduce_pass(s, h, k)
+        yield
+        for h in (0, 1):
+            reduce_end(s, h, 2)
+            reduce_send(s, h, None)
+        yield
+        for h in (0, 1):
+            reduce_end(s, h, -1)
+            reduce_end(s, h, 1)
+        for h in (0, 1):
+            reduce_pass(s, h, None)
+        yield
+        for h in (0, 1):
+            reduce_end(s, h, 0)
+        yield
+        for h in (0, 1):
+            reduce_end(s, h, None)
+        yield
+
+    def project(g):
+        acc_ref[g] = lax.dot_general(dq_ref[...], wq_ref[g], LAST, preferred_element_type=jnp.float32)
+
+    far = 40 * PARTS
+
+    def rows_of(s, h):
+        return pl.ds(h * half + s * size, size)
+
+    def spread(s, step):
+        n = s * 4 + RS_ORDER.index(step)
+        other, mine = tp_place(step, 1 - core), tp_place(step, core)
+        for h in (0, 1):
+            low = sum_ref[rows_of(s, h), :]
+            pair_out[n, h] = (acc_ref[other, rows_of(s, h), :] + lax.dot_general(
+                low, wkv_ref[other], LAST, preferred_element_type=jnp.float32)).astype(jnp.bfloat16)
+        begin(("pair", n), far + n, {"tp": tp_place(0, 1 - core)}, pair_out.at[n], pair_in.at[n])
+        for h in (0, 1):
+            low = sum_ref[rows_of(s, h), :]
+            acc_ref[mine, rows_of(s, h), :] += lax.dot_general(
+                low, wkv_ref[mine], LAST, preferred_element_type=jnp.float32)
+
+    def chip_sum(s, step, h):
+        n = s * 4 + RS_ORDER.index(step)
+        return acc_ref[tp_place(step, core), rows_of(s, h), :] + wide(pair_in[n, h])
+
+    def y_send(s):
+        copies["pair", s * 4].wait_recv()
+        for h in (0, 1):
+            y_stage[s, 0, h] = chip_sum(s, 2, h).astype(jnp.bfloat16)
+        number = far + 4 * PARTS + 4 * s
+        begin(("y_low", s), number, {"tp": tp_place(1, core)}, y_stage.at[s, 0, 0], y_low.at[s])
+        begin(("y_high", s), number + 1, {"tp": tp_place(-1, core)}, y_stage.at[s, 0, 1], y_high.at[s])
+
+    def y_pass(s, step):
+        number = far + 4 * PARTS + 4 * s
+        copies["pair", s * 4 + RS_ORDER.index(step)].wait_recv()
+        slot, low = (1, 0) if step == 1 else (2, 1)
+        y_stage[s, slot, 1 - low] = chip_sum(s, step, 1 - low).astype(jnp.bfloat16)
+        copies["y_low" if step == 1 else "y_high", s].wait_recv()
+        came = y_low if step == 1 else y_high
+        y_stage[s, slot, low] = (chip_sum(s, step, low) + wide(came[s])).astype(jnp.bfloat16)
+        begin(("y_fin", s, step), number + 1 + slot, {"tp": tp_place(step, core)}, y_stage.at[s, slot],
+              y_fin.at[s, slot - 1])
+
+    def y_end(s):
+        copies["pair", s * 4 + 3].wait_recv()
+        copies["y_fin", s, 1].wait_recv()
+        copies["y_fin", s, -1].wait_recv()
+        for h in (0, 1):
+            out_ref[rows_of(s, h), :] = (
+                chip_sum(s, 0, h) + wide(y_fin[s, 0, h]) + wide(y_fin[s, 1, h])).astype(jnp.bfloat16)
+
+    for copy in loads[:1]:
+        copy.wait()
+    first, second = reduce_steps(0), reduce_steps(1)
+    next(first)
+    loads[1].wait()
+    for g in (0, 1):
+        project(g)
+    next(first)
+    next(second)
+    for g in (2, 3):
+        project(g)
+    next(first)
+    project(4)
+    next(first)
+    project(5)
+    next(first)
+    for g in (6, 7):
+        project(g)
+    loads[2].wait()
+    loads[3].wait()
+    next(first)
+    spread(0, 2)
+    next(second)
+    spread(0, 1)
+    y_send(0)
+    spread(0, -1)
+    next(second)
+    spread(0, 0)
+    y_pass(0, 1)
+    y_pass(0, -1)
+    next(second)
+    next(second)
+    next(second)
+    spread(1, 2)
+    spread(1, 1)
+    y_send(1)
+    spread(1, -1)
+    spread(1, 0)
+    y_end(0)
+    y_pass(1, 1)
+    y_pass(1, -1)
+    y_end(1)
+    for copy in copies.values():
+        copy.wait_send()
+
+
+def finish(query_grad, terms, w_query, w_key, w_value):
+    rows = query_grad.shape[0]
+    blocks = SIDE * 2
+    columns = w_query.shape[0] // blocks
+    size = rows // 2 // PARTS
+    mid = size // 2
+    reduces = 10 * PARTS
+    sems = 4 * reduces + 8 * PARTS
+    bf = jnp.bfloat16
+    vmem = pl.BlockSpec(memory_space=pltpu.VMEM)
+    anywhere = pl.BlockSpec(memory_space=pl.ANY)
+    return pl.pallas_call(
+        finish_kernel,
+        out_shape=jax.ShapeDtypeStruct((rows, columns), bf),
+        in_specs=[vmem] + [anywhere] * 4,
+        out_specs=vmem,
+        scratch_shapes=[
+            pltpu.VMEM(terms.shape, bf),
+            pltpu.VMEM((blocks, columns, w_query.shape[1]), bf),
+            pltpu.VMEM((blocks, columns, 2 * HD), bf),
+            pltpu.VMEM((blocks, rows, columns), jnp.float32),
+            pltpu.VMEM((rows, 2 * HD), bf),
+            pltpu.VMEM((reduces, mid, 2 * HD), bf),
+            pltpu.VMEM((reduces, mid, 2 * HD), bf),
+            pltpu.VMEM((reduces, 2, size, 2 * HD), bf),
+            pltpu.VMEM((reduces, 2, size, 2 * HD), bf),
+            pltpu.VMEM((PARTS, 2, 4, size, 2 * HD), bf),
+            pltpu.VMEM((4 * PARTS, 2, size, columns), bf),
+            pltpu.VMEM((4 * PARTS, 2, size, columns), bf),
+            pltpu.VMEM((PARTS, 3, 2, size, columns), bf),
+            pltpu.VMEM((PARTS, size, columns), bf),
+            pltpu.VMEM((PARTS, size, columns), bf),
+            pltpu.VMEM((PARTS, 2, 2, size, columns), bf),
+            pltpu.SemaphoreType.DMA((4,)),
+            pltpu.SemaphoreType.DMA((sems,)),
+            pltpu.SemaphoreType.DMA((sems,)),
+        ],
+        compiler_params=pltpu.CompilerParams(collective_id=1, has_side_effects=True, vmem_limit_bytes=60 * 2**20),
+        name="finish",
+    )(query_grad, terms, w_query.reshape(blocks, columns, -1), w_key.reshape(blocks, columns, -1),
+      w_value.reshape(blocks, columns, -1))
 
 
 def shards(queries, keys, values, outputs, out_grad, lengths, w_query, w_key, w_value):
-    row_count = queries.shape[0]
-    heads = queries.shape[1] // HD
+    rows = queries.shape[0]
     me = lax.axis_index("ctx")
-    starts = me * row_count + jnp.arange(row_count // CHUNK, dtype=jnp.int32) * CHUNK
-    delta = jnp.sum(
-        (out_grad.astype(jnp.float32) * outputs.astype(jnp.float32)).reshape(row_count, heads, HD), axis=2
-    ).T
-    collected = lax.all_gather(jnp.stack([keys, values]), "ctx", axis=1, tiled=True)
-    query_grad, key_terms, value_terms = attention(
-        starts, lengths, queries, out_grad, delta, collected[0], collected[1]
-    )
-    devices = lax.axis_size("ctx")
-    partials = jnp.stack(
-        [key_terms.reshape(devices, row_count, HD), value_terms.reshape(devices, row_count, HD)], axis=1
-    )
-    summed = lax.psum_scatter(partials, "ctx", scatter_dimension=0, tiled=True)[0]
-    contract = (((1,), (1,)), ((), ()))
-    total = lax.dot_general(query_grad, w_query, contract, preferred_element_type=jnp.float32)
-    total = total + lax.dot_general(summed[0], w_key, contract, preferred_element_type=jnp.float32)
-    total = total + lax.dot_general(summed[1], w_value, contract, preferred_element_type=jnp.float32)
-    return lax.psum_scatter(total.astype(jnp.bfloat16), "tp", scatter_dimension=1, tiled=True)
+    starts = me * rows + jnp.arange(rows // CHUNK, dtype=jnp.int32) * CHUNK
+    collected, delta = collect(keys, values, out_grad, outputs)
+    query_grad, terms = attention(starts, lengths, queries, out_grad, delta, collected.reshape(-1, 2 * HD))
+    return finish(query_grad, terms.reshape(collected.shape), w_query, w_key, w_value)
 
 
 def solution(mesh):

time: 346 us -> 193 us (0.56)
  waiting for transfers between devices: 260 us -> 0 us
  Pallas kernels: 19.6 us -> 183 us
  matrix products: 24.2 us -> 0 us
  between operations: 13.2 us -> 0.03 us
  other arithmetic: 10.2 us -> 0.59 us
  local copies, waits for them, and re-layouts: 18 us -> 8.82 us
    unnamed x5 -> x0, waiting for transfers between devices: 211 us -> none
    pallas_call x0 -> x2, Pallas kernels: none -> 163 us  [the longest x1 133 us: finish(): pl.pallas_call(finish_kernel, out_shape=jax.ShapeDtypeStruct((rows, colum...]
    all_gather x1 -> x0, waiting for transfers between devices: 49.4 us -> none  [shards(): lax.all_gather(jnp.stack([keys, values]), 'ctx', axis=1, tiled=True)]
    dot_general x3 -> x0, matrix products: 24.2 us -> none  [the longest x1 12.1 us: shards(): lax.dot_general(query_grad, w_query, contract, preferred_element_type=jnp...]
    another operation x2 -> x0, other arithmetic: 6.46 us -> none  [the longest x1 4.66 us: shards(): jnp.stack([key_terms.reshape(devices, row_count, HD), value_terms.reshape...]
    squeeze x1 -> x0, local copies, waits for them, and re-layouts: 4.48 us -> none  [shards(): collected[1]]
    unnamed x14 -> x13, local copies, waits for them, and re-layouts: 11.8 us -> 8.82 us
  transfers between devices with their start and end apart: 3 -> 0, of which waited for: 3 -> 0; matrix products, arithmetic and copies ran while one was open for 5% -> 0% of each run, Pallas kernels for 0% -> 0%
where the time goes in v2:
time: 193 us; the launch traced here: 192 us
  Pallas kernels  183 us (95%)
  local copies, waits for them, and re-layouts  8.82 us (5%)
    pallas_call x1, Pallas kernels, finish(): pl.pallas_call(finish_kernel, out_shape=jax.ShapeDtypeStruct((rows, colum...  133 us
    pallas_call x1, Pallas kernels, collect(): pl.pallas_call(collect_kernel, out_shape=[jax.ShapeDtypeStruct((SIDE * SI...  30.1 us
    pallas_call x1, Pallas kernels, attention(): pl.pallas_call(functools.partial(attention_kernel, total), out_shape=[jax...  19.9 us
    unnamed x13, local copies, waits for them, and re-layouts  8.82 us

profile of v2, /device:TPU:0, one launch (start us, length us, event | category | flops | bytes accessed | tf_op | source)
XLA Modules:
  0.0 192.2 jit_solution(613452326972519262)
XLA Ops:
  0.0 0.6 multiply_add_fusion.start_ref
  0.6 0.0 copy-start.1
  0.6 1.2 copy-done.1
  1.8 0.0 copy-start.2
  1.8 1.2 copy-done.2
  3.0 0.0 copy-start.3
  3.0 0.9 copy-done.3
  4.0 0.0 copy-start.4
  4.0 0.9 copy-done.4
  4.9 30.1 %collect.1 = (bf16[16,512,256]{2,1,0:T(8,128)(2,1)S(1)}, f32[8,512]{1,0:T(8,128)S(1)}) custom-call(bf16[512,128]{1,0:T(8,128)(2,1)S(1)} %copy-done.3, bf16[512,128]{1,0:T(8,128)(2,1)S(1)} %copy-done.4, bf16[512,1024]{1,0:T(8,128)(2,1)S(1)} %copy-done.1, bf16[512,1024]{1,0:T(8,128)(2,1)S(1)} %copy-done.2), custom_call_target="tpu_custom_call" | custom-call | tf_op jit(solution)/shard_map/collect/pallas_call | solution.py:306
  34.9 0.0 copy-start
  34.9 2.0 %copy-done = bf16[16,512,256]{2,1,0:T(8,128)(2,1)} copy-done((bf16[16,512,256]{2,1,0:T(8,128)(2,1)}, bf16[16,512,256]{2,1,0:T(8,128)(2,1)S(1)}, u32[]{:S(2)}) %copy-start) | copy-done | bytes 4194328
  36.9 0.0 copy-start.5
  36.9 0.6 copy-done.5
  37.5 19.9 %attention.1 = (bf16[512,1024]{1,0:T(8,128)(2,1)}, bf16[8192,256]{1,0:T(8,128)(2,1)}) custom-call(s32[4]{0:T(128)} %multiply_add_fusion.start_ref, s32[8]{0:T(128)} %lengths_ref.1, bf16[512,1024]{1,0:T(8,128)(2,1)} %q_ref.1, bf16[512,1024]{1,0:T(8,128)(2,1)} %do_ref.1, f32[8,512]{1,0:T(8,128)} %copy-done.5, bf16[8192,256]{1,0:T(8,128)(2,1)} %bitcast.5), custom_call_target="tpu_custom_call" | custom-call | tf_op jit(solution)/shard_map/attention/pallas_call | solution.py:177
  57.4 132.8 %finish.1 = bf16[512,640]{1,0:T(8,128)(2,1)} custom-call(bf16[512,1024]{1,0:T(8,128)(2,1)} %get-tuple-element.11.dq_ref, bf16[16,512,256]{2,1,0:T(8,128)(2,1)} %bitcast.7, bf16[8,640,1024]{2,1,0:T(8,128)(2,1)} %bitcast.6, bf16[8,640,128]{2,1,0:T(8,128)(2,1)} %bitcast.8, bf16[8,640,128]{2,1,0:T(8,128)(2,1)} %bitcast.9), custom_call_target="tpu_custom_call" | custom-call | tf_op jit(solution)/shard_map/finish/pallas_call | solution.py:528
  190.2 2.0 %copy.11 = bf16[512,640]{1,0:T(8,128)(2,1)} copy(bf16[512,640]{1,0:T(8,128)(2,1)} %finish.1) | data formatting | bytes 1310720
Async XLA Ops:
  0.6 1.2 copy-start.1
  1.8 1.2 copy-start.2
  3.0 0.9 copy-start.3
  4.0 0.9 copy-start.4
  34.9 2.0 %copy-start = (bf16[16,512,256]{2,1,0:T(8,128)(2,1)}, bf16[16,512,256]{2,1,0:T(8,128)(2,1)S(1)}, u32[]{:S(2)}) copy-start(bf16[16,512,256]{2,1,0:T(8,128)(2,1)S(1)} %get-tuple-element.10) | copy-start | bytes 12582916
  36.9 0.6 copy-start.5

commit v3 on v2

--- a/solution.py
+++ b/solution.py
@@ -13,8 +13,11 @@
 LAST = (((1,), (1,)), ((), ()))
 
 
-def attention_kernel(total, start_ref, lengths_ref, q_ref, do_ref, delta_ref, kv_ref,
-                     dq_ref, dkv_ref, e_ref, ds_ref, mt_ref, q_rows, do_rows, q_over, do_over, kt_ref, dqt_ref,
+PIECES = 4
+
+
+def attention_kernel(total, start_ref, lengths_ref, row_ref, q_hbm, do_hbm, kv_hbm,
+                     dq_hbm, dkv_hbm, q_ref, do_ref, kv_ref, dq_ref, dkv_ref, load_sem, store_sem, e_ref, ds_ref, mt_ref, q_rows, do_rows, q_over, do_over, kt_ref, dqt_ref,
                      dk_acc, dv_acc, stat_ref):
     rows = q_rows.shape[0]
     heads = rows // CHUNK
@@ -25,8 +28,21 @@
     scale = HD ** -0.5
     to_log2 = scale * 1.4426950408889634
 
-    dk_acc[...] = jnp.zeros_like(dk_acc)
-    dv_acc[...] = jnp.zeros_like(dv_acc)
+    piece = total // PIECES
+    loads = [pltpu.make_async_copy(kv_hbm.at[pl.ds(n * piece, piece), :], kv_ref.at[pl.ds(n * piece, piece), :],
+                                   load_sem.at[n]) for n in range(PIECES)]
+    loads += [pltpu.make_async_copy(q_hbm, q_ref, load_sem.at[PIECES]),
+              pltpu.make_async_copy(do_hbm, do_ref, load_sem.at[PIECES + 1])]
+    for copy in loads:
+        copy.start()
+
+    def clear(i, _):
+        at = pl.ds(pl.multiple_of(i * TILE, TILE), TILE)
+        dk_acc[at, :] = jnp.zeros((TILE, HD), jnp.float32)
+        dv_acc[at, :] = jnp.zeros((TILE, HD), jnp.float32)
+        return 0
+
+    lax.fori_loop(0, tiles, clear, 0)
 
     def turn_keys(i, most):
         turned = kv_ref[pl.ds(pl.multiple_of(i * TILE, TILE), TILE), :HD].T
@@ -34,19 +50,22 @@
         wide = turned.astype(jnp.float32)
         return jnp.maximum(most, jnp.sum(wide * wide, axis=0, keepdims=True))
 
-    key_most = jnp.max(lax.fori_loop(0, tiles, turn_keys, jnp.zeros((1, TILE), jnp.float32)))
+    key_most = jnp.zeros((1, TILE), jnp.float32)
+    for n in range(PIECES):
+        loads[n].wait()
+        key_most = lax.fori_loop(n * tiles // PIECES, (n + 1) * tiles // PIECES, turn_keys, key_most, unroll=4)
+    key_most = jnp.max(key_most)
+    for copy in loads[PIECES:]:
+        copy.wait()
 
     def one_chunk(j, _):
         first = start_ref[j]
         t0 = pl.multiple_of(j * CHUNK, CHUNK)
-        query_most = jnp.zeros((CHUNK, 1), jnp.float32)
         for h in range(heads):
             part = q_ref[pl.ds(t0, CHUNK), h * HD:(h + 1) * HD]
             q_rows[h * CHUNK:(h + 1) * CHUNK, :] = part
             do_rows[h * CHUNK:(h + 1) * CHUNK, :] = do_ref[pl.ds(t0, CHUNK), h * HD:(h + 1) * HD]
-            wide = part.astype(jnp.float32)
-            query_most = jnp.maximum(query_most, jnp.sum(wide * wide, axis=1, keepdims=True))
-        small = jnp.max(query_most) * key_most * (to_log2 * to_log2) <= SAFE * SAFE
+        small = jnp.max(row_ref[heads:, pl.ds(t0, CHUNK)]) * key_most * (to_log2 * to_log2) <= SAFE * SAFE
         query_pos = first + lax.broadcasted_iota(jnp.int32, (1, pair), 1) % CHUNK
         row_start = jnp.zeros((1, pair), jnp.int32)
         low, high = jnp.int32(0), jnp.int32(0)
@@ -132,8 +151,8 @@
             inverse = jnp.broadcast_to(stat_ref[:, part], (HD, CHUNK)).T
             q_over[part, :] = (q_rows[part, :].astype(jnp.float32) * inverse).astype(jnp.bfloat16)
             do_over[part, :] = (do_rows[part, :].astype(jnp.float32) * inverse).astype(jnp.bfloat16)
-        delta = [jnp.concatenate([delta_ref[2 * p:2 * p + 1, pl.ds(t0, CHUNK)],
-                                  delta_ref[2 * p + 1:2 * p + 2, pl.ds(t0, CHUNK)]], axis=1) for p in range(pairs)]
+        delta = [jnp.concatenate([row_ref[2 * p:2 * p + 1, pl.ds(t0, CHUNK)],
+                                  row_ref[2 * p + 1:2 * p + 2, pl.ds(t0, CHUNK)]], axis=1) for p in range(pairs)]
         dqt_ref[...] = jnp.zeros_like(dqt_ref)
 
         def grad_step(i, _):
@@ -155,6 +174,7 @@
             part = slice(h * CHUNK, (h + 1) * CHUNK)
             dq_ref[pl.ds(t0, CHUNK), h * HD:(h + 1) * HD] = (
                 dqt_ref[:, part] * (stat_ref[:, part] * scale)).T.astype(jnp.bfloat16)
+        pltpu.make_async_copy(dq_ref.at[pl.ds(t0, CHUNK), :], dq_hbm.at[pl.ds(t0, CHUNK), :], store_sem.at[j]).start()
         return 0
 
     lax.fori_loop(0, chunks, one_chunk, 0)
@@ -165,22 +185,40 @@
         dkv_ref[at, HD:] = dv_acc[at, :].astype(jnp.bfloat16)
         return 0
 
-    lax.fori_loop(0, tiles, write, 0)
-
-
-def attention(starts, lengths, q, do, delta, kv, longest=4608):
+    stores = []
+    for n in range(PIECES):
+        lax.fori_loop(n * tiles // PIECES, (n + 1) * tiles // PIECES, write, 0)
+        stores.append(pltpu.make_async_copy(dkv_ref.at[pl.ds(n * piece, piece), :],
+                                            dkv_hbm.at[pl.ds(n * piece, piece), :], store_sem.at[chunks + n]))
+        stores[-1].start()
+    for j in range(chunks):
+        part = pl.ds(j * CHUNK, CHUNK)
+        pltpu.make_async_copy(dq_ref.at[part, :], dq_hbm.at[part, :], store_sem.at[j]).wait()
+    for copy in stores:
+        copy.wait()
+
+
+def attention(starts, lengths, q, do, row_info, kv, longest=4608):
     total = kv.shape[0]
     rows = q.shape[1] // HD * CHUNK
     max_tiles = (longest + CHUNK) // TILE + 2
     vmem = pl.BlockSpec(memory_space=pltpu.VMEM)
     smem = pl.BlockSpec(memory_space=pltpu.SMEM)
+    anywhere = pl.BlockSpec(memory_space=pl.ANY)
     return pl.pallas_call(
         functools.partial(attention_kernel, total),
         out_shape=[jax.ShapeDtypeStruct(q.shape, jnp.bfloat16),
                    jax.ShapeDtypeStruct(kv.shape, jnp.bfloat16)],
-        in_specs=[smem, smem] + [vmem] * 4,
-        out_specs=[vmem] * 2,
+        in_specs=[smem, smem, vmem] + [anywhere] * 3,
+        out_specs=[anywhere] * 2,
         scratch_shapes=[
+            pltpu.VMEM(q.shape, jnp.bfloat16),
+            pltpu.VMEM(q.shape, jnp.bfloat16),
+            pltpu.VMEM(kv.shape, jnp.bfloat16),
+            pltpu.VMEM(q.shape, jnp.bfloat16),
+            pltpu.VMEM(kv.shape, jnp.bfloat16),
+            pltpu.SemaphoreType.DMA((PIECES + 2,)),
+            pltpu.SemaphoreType.DMA((q.shape[0] // CHUNK + PIECES,)),
             pltpu.VMEM((max_tiles, TILE, rows), jnp.bfloat16),
             pltpu.VMEM((TILE, rows), jnp.bfloat16),
             pltpu.VMEM((max_tiles, 1, rows), jnp.float32),
@@ -194,9 +232,9 @@
             pltpu.VMEM((total, HD), jnp.float32),
             pltpu.VMEM((1, rows), jnp.float32),
         ],
-        compiler_params=pltpu.CompilerParams(vmem_limit_bytes=60 * 2**20),
+        compiler_params=pltpu.CompilerParams(vmem_limit_bytes=62 * 2**20),
         name="attention",
-    )(starts, lengths, q, do, delta, kv)
+    )(starts, lengths, row_info, q, do, kv)
 
 
 SIDE = 4
@@ -207,7 +245,7 @@
     me = lax.axis_index("ctx")
     x, z = me // SIDE, me % SIDE
     if axis == 0:
-        return lax.rem(x + step + SIDE, SIDE) * SIDE + z
+        return lax.rem(x + step + 2 * SIDE, SIDE) * SIDE + z
     return x * SIDE + lax.rem(z + step + SIDE, SIDE)
 
 
@@ -225,62 +263,105 @@
     pl.semaphore_wait(barrier, len(partners))
 
 
-def collect_kernel(k_ref, v_ref, out_grad_ref, outputs_ref, kv_ref, delta_ref, local_sem, send_sem, recv_sem):
+RELAY = ((1, 0), (-1, 1))
+
+
+def collect_kernel(k_ref, v_ref, q_ref, out_grad_ref, outputs_ref, kv_ref, q_out, out_grad_out, row_out,
+                   q_vmem, out_grad_vmem, outputs_vmem, row_vmem, relay, local_sem, send_sem, recv_sem):
     me = lax.axis_index("ctx")
     rows = k_ref.shape[0]
     half = rows // 2
-    quarter = half // 2
+    mid = half // 2
+    quarter = rows // SIDE
     own = [
         pltpu.make_async_copy(k_ref, kv_ref.at[me, :, pl.ds(0, HD)], local_sem.at[0]),
         pltpu.make_async_copy(v_ref, kv_ref.at[me, :, pl.ds(HD, HD)], local_sem.at[1]),
     ]
-    for copy in own:
+    kept = [
+        pltpu.make_async_copy(q_ref, q_vmem, local_sem.at[2]),
+        pltpu.make_async_copy(out_grad_ref, out_grad_vmem, local_sem.at[3]),
+        pltpu.make_async_copy(outputs_ref, outputs_vmem, local_sem.at[4]),
+    ]
+    for copy in own + kept:
         copy.start()
-    greet([{"ctx": ring_place(axis, step)} for axis in (0, 1) for step in (1, -1)])
+    greet([{"ctx": ring_place(axis, step)} for axis, step in ((0, 1), (0, -1), (0, 2), (1, 1), (1, -1))])
     for copy in own:
         copy.wait()
     copies = {}
 
-    def begin(name, number, axis, step, block, start, count):
-        region = kv_ref.at[block, pl.ds(start, count), :]
+    def begin(name, number, place, src, dst):
         copy = pltpu.make_async_remote_copy(
-            src_ref=region, dst_ref=region, send_sem=send_sem.at[number], recv_sem=recv_sem.at[number],
-            device_id={"ctx": ring_place(axis, step)}, device_id_type=MESH)
+            src_ref=src, dst_ref=dst, send_sem=send_sem.at[number], recv_sem=recv_sem.at[number],
+            device_id={"ctx": ring_place(*place)}, device_id_type=MESH)
         copy.start()
         copies[name] = copy
 
+    def pass_on(name, number, place, block, start, count):
+        region = kv_ref.at[block, pl.ds(start, count), :]
+        begin(name, number, place, region, region)
+
     def near(h, item, shift):
-        axis = h if item == "line" else 1 - h
+        axis = 0 if item == "line" else 1
         base = h * 20 + (0 if item == "line" else 4 + 4 * item)
-        block = me if item == "line" else block_at(h, shift, 0)
-        begin((h, item, 0), base, axis, 1, block, h * half, half)
-        begin((h, item, 1), base + 1, axis, -1, block, h * half, half)
+        block = me if item == "line" else block_at(0, shift, 0)
+        pass_on((h, item, 0), base, (axis, 1), block, h * half, half)
+        pass_on((h, item, 1), base + 1, (axis, -1), block, h * half, half)
 
     def far(h, item, shift):
-        axis = h if item == "line" else 1 - h
+        axis = 0 if item == "line" else 1
         base = h * 20 + (0 if item == "line" else 4 + 4 * item)
 
         def block(step):
-            return block_at(h, step, 0) if item == "line" else block_at(h, shift, step)
+            return block_at(0, step, 0) if item == "line" else block_at(0, shift, step)
 
         copies[h, item, 0].wait_recv()
-        begin((h, item, 2), base + 2, axis, 1, block(-1), h * half, quarter)
+        pass_on((h, item, 2), base + 2, (axis, 1), block(-1), h * half, mid)
         copies[h, item, 1].wait_recv()
-        begin((h, item, 3), base + 3, axis, -1, block(1), h * half + quarter, quarter)
+        pass_on((h, item, 3), base + 3, (axis, -1), block(1), h * half + mid, mid)
 
     shifts = (0, -1, 1, 2)
+    pairs = ((q_ref, q_out), (out_grad_ref, out_grad_out))
     for h in (0, 1):
         near(h, "line", 0)
     for h in (0, 1):
         near(h, 0, shifts[0])
-    for head in range(delta_ref.shape[0]):
+    for n, (src, dst) in enumerate(pairs):
+        for step, slot in RELAY:
+            part = pl.ds(2 * quarter + slot * (quarter // 2), quarter // 2)
+            begin(("relay", n, slot), 40 + 2 * n + slot, (0, step), src.at[part, :], relay.at[n, slot])
+    for n, (src, dst) in enumerate(pairs):
+        for j, step in ((1, 1), (3, -1)):
+            part = pl.ds(j * quarter, quarter)
+            begin(("move", n, j), 44 + 2 * n + j // 2, (0, step), src.at[part, :], dst.at[part, :])
+    for copy in kept:
+        copy.wait()
+    stay = [
+        pltpu.make_async_copy(q_vmem.at[pl.ds(0, quarter), :], q_out.at[pl.ds(0, quarter), :], local_sem.at[0]),
+        pltpu.make_async_copy(out_grad_vmem.at[pl.ds(0, quarter), :], out_grad_out.at[pl.ds(0, quarter), :],
+                              local_sem.at[1]),
+    ]
+    for copy in stay:
+        copy.start()
+    heads = row_vmem.shape[0] // 2
+    for head in range(heads):
         part = slice(head * HD, (head + 1) * HD)
-        product = out_grad_ref[:, part].astype(jnp.float32) * outputs_ref[:, part].astype(jnp.float32)
-        delta_ref[head:head + 1, :] = jnp.sum(product.T, axis=0, keepdims=True)
+        grad = out_grad_vmem[:, part].astype(jnp.float32)
+        query = q_vmem[:, part].astype(jnp.float32)
+        row_vmem[head:head + 1, :] = jnp.sum((grad * outputs_vmem[:, part].astype(jnp.float32)).T, axis=0, keepdims=True)
+        row_vmem[heads + head:heads + head + 1, :] = jnp.sum((query * query).T, axis=0, keepdims=True)
+    for j, step in ((1, 1), (2, 2), (3, -1)):
+        part = pl.ds(j * quarter, quarter)
+        begin(("rows", j), 51 + j, (0, step), row_vmem.at[:, part], row_out.at[:, part])
+    row_out[:, :quarter] = row_vmem[:, :quarter]
     for h in (0, 1):
         far(h, "line", 0)
         near(h, 1, shifts[1])
         near(h, 2, shifts[2])
+    for n, (src, dst) in enumerate(pairs):
+        for step, slot in RELAY:
+            part = pl.ds(2 * quarter + slot * (quarter // 2), quarter // 2)
+            copies["relay", n, slot].wait_recv()
+            begin(("relayed", n, slot), 48 + 2 * n + slot, (0, step), relay.at[n, slot], dst.at[part, :])
     for h in (0, 1):
         far(h, 0, shifts[0])
     for h in (0, 1):
@@ -294,28 +375,43 @@
         for h in (0, 1):
             copies[h, item, 2].wait_recv()
             copies[h, item, 3].wait_recv()
+    for n in (0, 1):
+        for name in (("move", n, 1), ("move", n, 3), ("relayed", n, 0), ("relayed", n, 1)):
+            copies[name].wait_recv()
+    for j in (1, 2, 3):
+        copies["rows", j].wait_recv()
+    for copy in stay:
+        copy.wait()
     for copy in copies.values():
         copy.wait_send()
 
 
-def collect(keys, values, out_grad, outputs):
+def collect(keys, values, queries, out_grad, outputs):
     rows = keys.shape[0]
     heads = out_grad.shape[1] // HD
+    bf = jnp.bfloat16
     vmem = pl.BlockSpec(memory_space=pltpu.VMEM)
     anywhere = pl.BlockSpec(memory_space=pl.ANY)
     return pl.pallas_call(
         collect_kernel,
-        out_shape=[jax.ShapeDtypeStruct((SIDE * SIDE, rows, 2 * HD), jnp.bfloat16),
-                   jax.ShapeDtypeStruct((heads, rows), jnp.float32)],
-        in_specs=[anywhere, anywhere, vmem, vmem],
-        out_specs=[anywhere, vmem],
-        scratch_shapes=[pltpu.SemaphoreType.DMA((2,)), pltpu.SemaphoreType.DMA((40,)), pltpu.SemaphoreType.DMA((40,))],
-        compiler_params=pltpu.CompilerParams(collective_id=0, has_side_effects=True, vmem_limit_bytes=32 * 2**20),
+        out_shape=[jax.ShapeDtypeStruct((SIDE * SIDE, rows, 2 * HD), bf),
+                   jax.ShapeDtypeStruct(queries.shape, bf),
+                   jax.ShapeDtypeStruct(queries.shape, bf),
+                   jax.ShapeDtypeStruct((2 * heads, rows), jnp.float32)],
+        in_specs=[anywhere] * 5,
+        out_specs=[anywhere] * 3 + [vmem],
+        scratch_shapes=[pltpu.VMEM(queries.shape, bf), pltpu.VMEM(queries.shape, bf), pltpu.VMEM(queries.shape, bf),
+                        pltpu.VMEM((2 * heads, rows), jnp.float32),
+                        pltpu.VMEM((2, 2, rows // SIDE // 2, queries.shape[1]), bf),
+                        pltpu.SemaphoreType.DMA((5,)), pltpu.SemaphoreType.DMA((55,)), pltpu.SemaphoreType.DMA((55,))],
+        compiler_params=pltpu.CompilerParams(collective_id=0, has_side_effects=True, vmem_limit_bytes=62 * 2**20),
         name="collect",
-    )(keys, values, out_grad, outputs)
-
-
-PARTS = 2
+    )(keys, values, queries, out_grad, outputs)
+
+
+PARTS = 4
+PART_ORDER = (0, 1, 3, 2)
+FIRST_AXIS = ((0, 0), (0, 0), (0, 1), (0, 1))
 RS_ORDER = (2, -1, 1, 0)
 
 
@@ -324,19 +420,20 @@
     return lax.rem(y + step + SIDE, SIDE) * 2 + core
 
 
-def finish_kernel(dq_ref, dkv_hbm, wq_hbm, wk_hbm, wv_hbm, out_ref, dkv_ref, wq_ref, wkv_ref, acc_ref, sum_ref,
+def finish_kernel(dq_hbm, dkv_hbm, wq_hbm, wk_hbm, wv_hbm, out_ref, dq_ref, relay, dkv_ref, wq_ref, wkv_ref, acc_ref, sum_ref,
                   low_ref, high_ref, stage_ref, fin_ref, res_ref, pair_out, pair_in, y_stage, y_low, y_high, y_fin,
                   load_sem, send_sem, recv_sem):
     core = lax.axis_index("tp") % 2
     rows = dq_ref.shape[0]
-    half = rows // 2
-    size = half // PARTS
+    part_rows = rows // PARTS
+    size = part_rows // 2
     mid = size // 2
     loads = [
         pltpu.make_async_copy(dkv_hbm, dkv_ref, load_sem.at[0]),
         pltpu.make_async_copy(wq_hbm, wq_ref, load_sem.at[1]),
         pltpu.make_async_copy(wk_hbm, wkv_ref.at[:, :, pl.ds(0, HD)], load_sem.at[2]),
         pltpu.make_async_copy(wv_hbm, wkv_ref.at[:, :, pl.ds(HD, HD)], load_sem.at[3]),
+        pltpu.make_async_copy(dq_hbm.at[pl.ds(0, part_rows), :], dq_ref.at[pl.ds(0, part_rows), :], load_sem.at[4]),
     ]
     for copy in loads:
         copy.start()
@@ -353,24 +450,27 @@
     def wide(value):
         return value.astype(jnp.float32)
 
+    def rows_of(s, h):
+        return pl.ds(s * part_rows + h * size, size)
+
     def ident(s, h, k):
         return (s * 2 + h) * 5 + (4 if k is None else RS_ORDER.index(k))
 
     def term(s, h, k, shift, start, count):
         if k is None:
             return res_ref.at[s, h, RS_ORDER.index(shift), pl.ds(start, count), :]
-        return dkv_ref.at[block_at(h, k, shift), pl.ds(h * half + s * size + start, count), :]
-
-    def ring_axis(h, k):
-        return h if k is None else 1 - h
+        return dkv_ref.at[block_at(FIRST_AXIS[s][h], k, shift), pl.ds(s * part_rows + h * size + start, count), :]
+
+    def ring_axis(s, h, k):
+        return FIRST_AXIS[s][h] if k is None else 1 - FIRST_AXIS[s][h]
 
     def reduce_send(s, h, k):
-        n, axis = ident(s, h, k), ring_axis(h, k)
+        n, axis = ident(s, h, k), ring_axis(s, h, k)
         begin(("low", n), 4 * n, {"ctx": ring_place(axis, 1)}, term(s, h, k, 2, 0, mid), low_ref.at[n])
         begin(("high", n), 4 * n + 1, {"ctx": ring_place(axis, -1)}, term(s, h, k, 2, mid, mid), high_ref.at[n])
 
     def reduce_pass(s, h, k):
-        n, axis = ident(s, h, k), ring_axis(h, k)
+        n, axis = ident(s, h, k), ring_axis(s, h, k)
         copies["low", n].wait_recv()
         stage_ref[n, 0, :mid, :] = (wide(term(s, h, k, 1, 0, mid)[...]) + wide(low_ref[n])).astype(jnp.bfloat16)
         stage_ref[n, 0, mid:, :] = term(s, h, k, 1, mid, mid)[...]
@@ -386,7 +486,7 @@
         copies["down", n].wait_recv()
         total = wide(term(s, h, k, 0, 0, size)[...]) + wide(fin_ref[n, 0]) + wide(fin_ref[n, 1])
         if k is None:
-            sum_ref[pl.ds(h * half + s * size, size), :] = total.astype(jnp.bfloat16)
+            sum_ref[rows_of(s, h), :] = total.astype(jnp.bfloat16)
         else:
             res_ref[s, h, RS_ORDER.index(k)] = total.astype(jnp.bfloat16)
 
@@ -416,13 +516,27 @@
             reduce_end(s, h, None)
         yield
 
-    def project(g):
-        acc_ref[g] = lax.dot_general(dq_ref[...], wq_ref[g], LAST, preferred_element_type=jnp.float32)
+    def project(g, n):
+        part = pl.ds(n * (rows // 2), rows // 2)
+        acc_ref[g, part, :] = lax.dot_general(dq_ref[part, :], wq_ref[g], LAST, preferred_element_type=jnp.float32)
+
+    back = 48 * PARTS
+
+    def give_back():
+        for step, slot in RELAY:
+            part = pl.ds(2 * part_rows + slot * size, size)
+            begin(("relay", slot), back + slot, {"ctx": ring_place(0, step)}, dq_hbm.at[part, :], relay.at[slot])
+        for j, step in ((1, -1), (3, 1)):
+            part = pl.ds(j * part_rows, part_rows)
+            begin(("back", j), back + 2 + j // 2, {"ctx": ring_place(0, step)}, dq_hbm.at[part, :], dq_ref.at[part, :])
+
+    def relay_back():
+        for step, slot in RELAY:
+            part = pl.ds(2 * part_rows + slot * size, size)
+            copies["relay", slot].wait_recv()
+            begin(("relayed", slot), back + 4 + slot, {"ctx": ring_place(0, step)}, relay.at[slot], dq_ref.at[part, :])
 
     far = 40 * PARTS
-
-    def rows_of(s, h):
-        return pl.ds(h * half + s * size, size)
 
     def spread(s, step):
         n = s * 4 + RS_ORDER.index(step)
@@ -468,48 +582,75 @@
             out_ref[rows_of(s, h), :] = (
                 chip_sum(s, 0, h) + wide(y_fin[s, 0, h]) + wide(y_fin[s, 1, h])).astype(jnp.bfloat16)
 
-    for copy in loads[:1]:
-        copy.wait()
-    first, second = reduce_steps(0), reduce_steps(1)
-    next(first)
+    give_back()
+    sums = {s: reduce_steps(s) for s in PART_ORDER}
+    one, two, three, four = PART_ORDER
+    loads[0].wait()
+    next(sums[one])
+    relay_back()
+    next(sums[one])
+    next(sums[two])
+    copies["back", 1].wait_recv()
+    loads[4].wait()
     loads[1].wait()
-    for g in (0, 1):
-        project(g)
-    next(first)
-    next(second)
-    for g in (2, 3):
-        project(g)
-    next(first)
-    project(4)
-    next(first)
-    project(5)
-    next(first)
-    for g in (6, 7):
-        project(g)
+    for g in range(4):
+        project(g, 0)
+    next(sums[one])
+    next(sums[two])
+    next(sums[three])
+    for g in range(4, 8):
+        project(g, 0)
+    next(sums[one])
+    next(sums[one])
+    next(sums[two])
     loads[2].wait()
     loads[3].wait()
-    next(first)
-    spread(0, 2)
-    next(second)
-    spread(0, 1)
-    y_send(0)
-    spread(0, -1)
-    next(second)
-    spread(0, 0)
-    y_pass(0, 1)
-    y_pass(0, -1)
-    next(second)
-    next(second)
-    next(second)
-    spread(1, 2)
-    spread(1, 1)
-    y_send(1)
-    spread(1, -1)
-    spread(1, 0)
-    y_end(0)
-    y_pass(1, 1)
-    y_pass(1, -1)
-    y_end(1)
+    next(sums[one])
+    for step in RS_ORDER:
+        spread(one, step)
+    next(sums[three])
+    next(sums[four])
+    next(sums[two])
+    y_send(one)
+    copies["back", 3].wait_recv()
+    copies["relayed", 0].wait_recv()
+    copies["relayed", 1].wait_recv()
+    for g in range(4):
+        project(g, 1)
+    next(sums[two])
+    y_pass(one, 1)
+    y_pass(one, -1)
+    next(sums[two])
+    next(sums[three])
+    for step in RS_ORDER:
+        spread(two, step)
+    for g in range(4, 8):
+        project(g, 1)
+    next(sums[three])
+    next(sums[four])
+    y_send(two)
+    next(sums[three])
+    next(sums[four])
+    y_pass(two, 1)
+    y_pass(two, -1)
+    next(sums[three])
+    for step in RS_ORDER:
+        spread(three, step)
+    next(sums[four])
+    y_send(three)
+    next(sums[four])
+    next(sums[four])
+    for step in RS_ORDER:
+        spread(four, step)
+    y_pass(three, 1)
+    y_pass(three, -1)
+    y_send(four)
+    y_end(one)
+    y_end(two)
+    y_pass(four, 1)
+    y_pass(four, -1)
+    y_end(three)
+    y_end(four)
     for copy in copies.values():
         copy.wait_send()
 
@@ -518,19 +659,21 @@
     rows = query_grad.shape[0]
     blocks = SIDE * 2
     columns = w_query.shape[0] // blocks
-    size = rows // 2 // PARTS
+    size = rows // PARTS // 2
     mid = size // 2
     reduces = 10 * PARTS
-    sems = 4 * reduces + 8 * PARTS
+    sems = 4 * reduces + 8 * PARTS + 6
     bf = jnp.bfloat16
     vmem = pl.BlockSpec(memory_space=pltpu.VMEM)
     anywhere = pl.BlockSpec(memory_space=pl.ANY)
     return pl.pallas_call(
         finish_kernel,
         out_shape=jax.ShapeDtypeStruct((rows, columns), bf),
-        in_specs=[vmem] + [anywhere] * 4,
+        in_specs=[anywhere] * 5,
         out_specs=vmem,
         scratch_shapes=[
+            pltpu.VMEM(query_grad.shape, bf),
+            pltpu.VMEM((2, size, query_grad.shape[1]), bf),
             pltpu.VMEM(terms.shape, bf),
             pltpu.VMEM((blocks, columns, w_query.shape[1]), bf),
             pltpu.VMEM((blocks, columns, 2 * HD), bf),
@@ -547,11 +690,11 @@
             pltpu.VMEM((PARTS, size, columns), bf),
             pltpu.VMEM((PARTS, size, columns), bf),
             pltpu.VMEM((PARTS, 2, 2, size, columns), bf),
-            pltpu.SemaphoreType.DMA((4,)),
+            pltpu.SemaphoreType.DMA((5,)),
             pltpu.SemaphoreType.DMA((sems,)),
             pltpu.SemaphoreType.DMA((sems,)),
         ],
-        compiler_params=pltpu.CompilerParams(collective_id=1, has_side_effects=True, vmem_limit_bytes=60 * 2**20),
+        compiler_params=pltpu.CompilerParams(collective_id=1, has_side_effects=True, vmem_limit_bytes=62 * 2**20),
         name="finish",
     )(query_grad, terms, w_query.reshape(blocks, columns, -1), w_key.reshape(blocks, columns, -1),
       w_value.reshape(blocks, columns, -1))
@@ -559,10 +702,9 @@
 
 def shards(queries, keys, values, outputs, out_grad, lengths, w_query, w_key, w_value):
     rows = queries.shape[0]
-    me = lax.axis_index("ctx")
-    starts = me * rows + jnp.arange(rows // CHUNK, dtype=jnp.int32) * CHUNK
-    collected, delta = collect(keys, values, out_grad, outputs)
-    query_grad, terms = attention(starts, lengths, queries, out_grad, delta, collected.reshape(-1, 2 * HD))
+    starts = jnp.stack([ring_place(0, -j) * rows + j * CHUNK for j in range(SIDE)]).astype(jnp.int32)
+    collected, q_work, grad_work, row_info = collect(keys, values, queries, out_grad, outputs)
+    query_grad, terms = attention(starts, lengths, q_work, grad_work, row_info, collected.reshape(-1, 2 * HD))
     return finish(query_grad, terms.reshape(collected.shape), w_query, w_key, w_value)
 
 

time: 193 us -> 180 us (0.933)
  Pallas kernels: 183 us -> 176 us
  local copies, waits for them, and re-layouts: 8.82 us -> 1.98 us
    pallas_call x1, Pallas kernels: 133 us -> 83.4 us  [finish(): pl.pallas_call(finish_kernel, out_shape=jax.ShapeDtypeStruct((rows, colum...]
    pallas_call x1, Pallas kernels: 30.1 us -> 57.4 us  [collect(): pl.pallas_call(collect_kernel, out_shape=[jax.ShapeDtypeStruct((SIDE * SI...]
    pallas_call x1, Pallas kernels: 19.9 us -> 35.2 us  [attention(): pl.pallas_call(functools.partial(attention_kernel, total), out_shape=[jax...]
    unnamed x13 -> x1, local copies, waits for them, and re-layouts: 8.82 us -> 1.98 us
where the time goes in v3:
time: 180 us; the launch traced here: 179 us
  Pallas kernels  176 us (98%)
  local copies, waits for them, and re-layouts  1.98 us (1%)
    pallas_call x1, Pallas kernels, finish(): pl.pallas_call(finish_kernel, out_shape=jax.ShapeDtypeStruct((rows, colum...  83.4 us
    pallas_call x1, Pallas kernels, collect(): pl.pallas_call(collect_kernel, out_shape=[jax.ShapeDtypeStruct((SIDE * SI...  57.4 us
    pallas_call x1, Pallas kernels, attention(): pl.pallas_call(functools.partial(attention_kernel, total), out_shape=[jax...  35.2 us

profile of v3, /device:TPU:0, one launch (start us, length us, event | category | flops | bytes accessed | tf_op | source)
XLA Modules:
  0.0 178.5 jit_solution(9573239638069503975)
XLA Ops:
  0.0 0.6 pad_add_fusion.start_ref
  0.6 57.4 %collect.1 = (bf16[16,512,256]{2,1,0:T(8,128)(2,1)}, bf16[512,1024]{1,0:T(8,128)(2,1)}, bf16[512,1024]{1,0:T(8,128)(2,1)}, f32[16,512]{1,0:T(8,128)}) custom-call(bf16[512,128]{1,0:T(8,128)(2,1)} %k_ref.1, bf16[512,128]{1,0:T(8,128)(2,1)} %v_ref.1, bf16[512,1024]{1,0:T(8,128)(2,1)} %q_ref.1, bf16[512,1024]{1,0:T(8,128)(2,1)} %out_grad_ref.1, ...), custom_call_target="tpu_custom_call" | custom-call | tf_op jit(solution)/shard_map/collect/pallas_call | solution.py:395
  58.0 35.2 %attention.1 = (bf16[512,1024]{1,0:T(8,128)(2,1)}, bf16[8192,256]{1,0:T(8,128)(2,1)}) custom-call(s32[4]{0:T(128)} %pad_add_fusion.start_ref, s32[8]{0:T(128)} %lengths_ref.1, f32[16,512]{1,0:T(8,128)} %get-tuple-element.11.row_ref, bf16[512,1024]{1,0:T(8,128)(2,1)} %get-tuple-element.12.q_hbm, bf16[512,1024]{1,0:T(8,128)(2,1)} %get-tuple-element.13.do_hbm, ...), custom_call_target="tpu_custom_call" | custom-call | tf_op jit(solution)/shard_map/attention/pallas_call | solution.py:208
  93.1 83.4 %finish.1 = bf16[512,640]{1,0:T(8,128)(2,1)} custom-call(bf16[512,1024]{1,0:T(8,128)(2,1)} %get-tuple-element.15.dq_hbm, bf16[16,512,256]{2,1,0:T(8,128)(2,1)} %bitcast.11, bf16[8,640,1024]{2,1,0:T(8,128)(2,1)} %bitcast.9, bf16[8,640,128]{2,1,0:T(8,128)(2,1)} %bitcast.12, bf16[8,640,128]{2,1,0:T(8,128)(2,1)} %bitcast.13), custom_call_target="tpu_custom_call" | custom-call | tf_op jit(solution)/shard_map/finish/pallas_call | solution.py:669
  176.6 2.0 %copy.11 = bf16[512,640]{1,0:T(8,128)(2,1)} copy(bf16[512,640]{1,0:T(8,128)(2,1)} %finish.1) | data formatting | bytes 1310720

commit v4 on v3

--- a/solution.py
+++ b/solution.py
@@ -266,16 +266,16 @@
 RELAY = ((1, 0), (-1, 1))
 
 
-def collect_kernel(k_ref, v_ref, q_ref, out_grad_ref, outputs_ref, kv_ref, q_out, out_grad_out, row_out,
-                   q_vmem, out_grad_vmem, outputs_vmem, row_vmem, relay, local_sem, send_sem, recv_sem):
+def collect_kernel(k_ref, v_ref, q_ref, out_grad_ref, outputs_ref, kv_hbm, q_out, out_grad_out, row_out,
+                   kv_ref, k_vmem, v_vmem, q_vmem, out_grad_vmem, outputs_vmem, row_vmem, relay, local_sem, out_sem, send_sem, recv_sem):
     me = lax.axis_index("ctx")
     rows = k_ref.shape[0]
     half = rows // 2
     mid = half // 2
     quarter = rows // SIDE
     own = [
-        pltpu.make_async_copy(k_ref, kv_ref.at[me, :, pl.ds(0, HD)], local_sem.at[0]),
-        pltpu.make_async_copy(v_ref, kv_ref.at[me, :, pl.ds(HD, HD)], local_sem.at[1]),
+        pltpu.make_async_copy(k_ref, k_vmem, local_sem.at[0]),
+        pltpu.make_async_copy(v_ref, v_vmem, local_sem.at[1]),
     ]
     kept = [
         pltpu.make_async_copy(q_ref, q_vmem, local_sem.at[2]),
@@ -284,9 +284,11 @@
     ]
     for copy in own + kept:
         copy.start()
-    greet([{"ctx": ring_place(axis, step)} for axis, step in ((0, 1), (0, -1), (0, 2), (1, 1), (1, -1))])
     for copy in own:
         copy.wait()
+    kv_ref[me, :, :HD] = k_vmem[...]
+    kv_ref[me, :, HD:] = v_vmem[...]
+    greet([{"ctx": ring_place(axis, step)} for axis, step in ((0, 1), (0, -1), (0, 2), (1, 1), (1, -1))])
     copies = {}
 
     def begin(name, number, place, src, dst):
@@ -319,12 +321,24 @@
         copies[h, item, 1].wait_recv()
         pass_on((h, item, 3), base + 3, (axis, -1), block(1), h * half + mid, mid)
 
+    stores = []
+
+    def keep(block, h):
+        region = pl.ds(h * half, half)
+        stores.append(pltpu.make_async_copy(kv_ref.at[block, region, :], kv_hbm.at[block, region, :],
+                                            out_sem.at[len(stores)]))
+        stores[-1].start()
+
     shifts = (0, -1, 1, 2)
     pairs = ((q_ref, q_out), (out_grad_ref, out_grad_out))
     for h in (0, 1):
         near(h, "line", 0)
     for h in (0, 1):
         near(h, 0, shifts[0])
+    for h in (0, 1):
+        far(h, "line", 0)
+        near(h, 1, shifts[1])
+        near(h, 2, shifts[2])
     for n, (src, dst) in enumerate(pairs):
         for step, slot in RELAY:
             part = pl.ds(2 * quarter + slot * (quarter // 2), quarter // 2)
@@ -342,6 +356,9 @@
     ]
     for copy in stay:
         copy.start()
+    for h in (0, 1):
+        for shift in (0, -1, 1):
+            keep(block_at(0, shift, 0), h)
     heads = row_vmem.shape[0] // 2
     for head in range(heads):
         part = slice(head * HD, (head + 1) * HD)
@@ -354,33 +371,35 @@
         begin(("rows", j), 51 + j, (0, step), row_vmem.at[:, part], row_out.at[:, part])
     row_out[:, :quarter] = row_vmem[:, :quarter]
     for h in (0, 1):
-        far(h, "line", 0)
-        near(h, 1, shifts[1])
-        near(h, 2, shifts[2])
+        far(h, 0, shifts[0])
+        keep(block_at(0, 0, 1), h)
+        keep(block_at(0, 0, -1), h)
+    for h in (0, 1):
+        copies[h, "line", 2].wait_recv()
+        copies[h, "line", 3].wait_recv()
+        near(h, 3, shifts[3])
+        keep(block_at(0, 2, 0), h)
     for n, (src, dst) in enumerate(pairs):
         for step, slot in RELAY:
             part = pl.ds(2 * quarter + slot * (quarter // 2), quarter // 2)
             copies["relay", n, slot].wait_recv()
             begin(("relayed", n, slot), 48 + 2 * n + slot, (0, step), relay.at[n, slot], dst.at[part, :])
-    for h in (0, 1):
-        far(h, 0, shifts[0])
-    for h in (0, 1):
-        copies[h, "line", 2].wait_recv()
-        copies[h, "line", 3].wait_recv()
-        near(h, 3, shifts[3])
     for item in (1, 2, 3):
         for h in (0, 1):
             far(h, item, shifts[item])
+            keep(block_at(0, shifts[item], 1), h)
+            keep(block_at(0, shifts[item], -1), h)
     for item in (0, 1, 2, 3):
         for h in (0, 1):
             copies[h, item, 2].wait_recv()
             copies[h, item, 3].wait_recv()
+            keep(block_at(0, shifts[item], 2), h)
     for n in (0, 1):
         for name in (("move", n, 1), ("move", n, 3), ("relayed", n, 0), ("relayed", n, 1)):
             copies[name].wait_recv()
     for j in (1, 2, 3):
         copies["rows", j].wait_recv()
-    for copy in stay:
+    for copy in stay + stores:
         copy.wait()
     for copy in copies.values():
         copy.wait_send()
@@ -400,10 +419,10 @@
                    jax.ShapeDtypeStruct((2 * heads, rows), jnp.float32)],
         in_specs=[anywhere] * 5,
         out_specs=[anywhere] * 3 + [vmem],
-        scratch_shapes=[pltpu.VMEM(queries.shape, bf), pltpu.VMEM(queries.shape, bf), pltpu.VMEM(queries.shape, bf),
+        scratch_shapes=[pltpu.VMEM((SIDE * SIDE, rows, 2 * HD), bf), pltpu.VMEM(keys.shape, bf), pltpu.VMEM(keys.shape, bf), pltpu.VMEM(queries.shape, bf), pltpu.VMEM(queries.shape, bf), pltpu.VMEM(queries.shape, bf),
                         pltpu.VMEM((2 * heads, rows), jnp.float32),
                         pltpu.VMEM((2, 2, rows // SIDE // 2, queries.shape[1]), bf),
-                        pltpu.SemaphoreType.DMA((5,)), pltpu.SemaphoreType.DMA((55,)), pltpu.SemaphoreType.DMA((55,))],
+                        pltpu.SemaphoreType.DMA((5,)), pltpu.SemaphoreType.DMA((2 * SIDE * SIDE,)), pltpu.SemaphoreType.DMA((55,)), pltpu.SemaphoreType.DMA((55,))],
         compiler_params=pltpu.CompilerParams(collective_id=0, has_side_effects=True, vmem_limit_bytes=62 * 2**20),
         name="collect",
     )(keys, values, queries, out_grad, outputs)
@@ -420,7 +439,7 @@
     return lax.rem(y + step + SIDE, SIDE) * 2 + core
 
 
-def finish_kernel(dq_hbm, dkv_hbm, wq_hbm, wk_hbm, wv_hbm, out_ref, dq_ref, relay, dkv_ref, wq_ref, wkv_ref, acc_ref, sum_ref,
+def finish_kernel(dq_in, dkv_hbm, wq_hbm, wk_hbm, wv_hbm, out_ref, dkv_ref, dq_ref, relay, wq_ref, wk_ref, wv_ref, wkv_ref, acc_ref, sum_ref,
                   low_ref, high_ref, stage_ref, fin_ref, res_ref, pair_out, pair_in, y_stage, y_low, y_high, y_fin,
                   load_sem, send_sem, recv_sem):
     core = lax.axis_index("tp") % 2
@@ -431,9 +450,9 @@
     loads = [
         pltpu.make_async_copy(dkv_hbm, dkv_ref, load_sem.at[0]),
         pltpu.make_async_copy(wq_hbm, wq_ref, load_sem.at[1]),
-        pltpu.make_async_copy(wk_hbm, wkv_ref.at[:, :, pl.ds(0, HD)], load_sem.at[2]),
-        pltpu.make_async_copy(wv_hbm, wkv_ref.at[:, :, pl.ds(HD, HD)], load_sem.at[3]),
-        pltpu.make_async_copy(dq_hbm.at[pl.ds(0, part_rows), :], dq_ref.at[pl.ds(0, part_rows), :], load_sem.at[4]),
+        pltpu.make_async_copy(wk_hbm, wk_ref, load_sem.at[2]),
+        pltpu.make_async_copy(wv_hbm, wv_ref, load_sem.at[3]),
+        pltpu.make_async_copy(dq_in.at[pl.ds(0, part_rows), :], dq_ref.at[pl.ds(0, part_rows), :], load_sem.at[4]),
     ]
     for copy in loads:
         copy.start()
@@ -525,10 +544,10 @@
     def give_back():
         for step, slot in RELAY:
             part = pl.ds(2 * part_rows + slot * size, size)
-            begin(("relay", slot), back + slot, {"ctx": ring_place(0, step)}, dq_hbm.at[part, :], relay.at[slot])
+            begin(("relay", slot), back + slot, {"ctx": ring_place(0, step)}, dq_in.at[part, :], relay.at[slot])
         for j, step in ((1, -1), (3, 1)):
             part = pl.ds(j * part_rows, part_rows)
-            begin(("back", j), back + 2 + j // 2, {"ctx": ring_place(0, step)}, dq_hbm.at[part, :], dq_ref.at[part, :])
+            begin(("back", j), back + 2 + j // 2, {"ctx": ring_place(0, step)}, dq_in.at[part, :], dq_ref.at[part, :])
 
     def relay_back():
         for step, slot in RELAY:
@@ -541,15 +560,13 @@
     def spread(s, step):
         n = s * 4 + RS_ORDER.index(step)
         other, mine = tp_place(step, 1 - core), tp_place(step, core)
-        for h in (0, 1):
-            low = sum_ref[rows_of(s, h), :]
-            pair_out[n, h] = (acc_ref[other, rows_of(s, h), :] + lax.dot_general(
-                low, wkv_ref[other], LAST, preferred_element_type=jnp.float32)).astype(jnp.bfloat16)
+        part = pl.ds(s * part_rows, part_rows)
+        low = sum_ref[part, :]
+        total = acc_ref[other, part, :] + lax.dot_general(low, wkv_ref[other], LAST, preferred_element_type=jnp.float32)
+        pair_out[n, 0] = total[:size].astype(jnp.bfloat16)
+        pair_out[n, 1] = total[size:].astype(jnp.bfloat16)
         begin(("pair", n), far + n, {"tp": tp_place(0, 1 - core)}, pair_out.at[n], pair_in.at[n])
-        for h in (0, 1):
-            low = sum_ref[rows_of(s, h), :]
-            acc_ref[mine, rows_of(s, h), :] += lax.dot_general(
-                low, wkv_ref[mine], LAST, preferred_element_type=jnp.float32)
+        acc_ref[mine, part, :] += lax.dot_general(low, wkv_ref[mine], LAST, preferred_element_type=jnp.float32)
 
     def chip_sum(s, step, h):
         n = s * 4 + RS_ORDER.index(step)
@@ -582,70 +599,79 @@
             out_ref[rows_of(s, h), :] = (
                 chip_sum(s, 0, h) + wide(y_fin[s, 0, h]) + wide(y_fin[s, 1, h])).astype(jnp.bfloat16)
 
-    give_back()
     sums = {s: reduce_steps(s) for s in PART_ORDER}
     one, two, three, four = PART_ORDER
     loads[0].wait()
     next(sums[one])
+    next(sums[two])
+    give_back()
+    next(sums[one])
+    next(sums[three])
+    next(sums[two])
+    next(sums[one])
     relay_back()
     next(sums[one])
-    next(sums[two])
+    loads[1].wait()
+    loads[4].wait()
     copies["back", 1].wait_recv()
-    loads[4].wait()
-    loads[1].wait()
-    for g in range(4):
+    for g in range(0, 4):
         project(g, 0)
     next(sums[one])
     next(sums[two])
     next(sums[three])
+    next(sums[four])
     for g in range(4, 8):
         project(g, 0)
-    next(sums[one])
+    loads[2].wait()
+    loads[3].wait()
+
+    def merge(g, _):
+        wkv_ref[g, :, :HD] = wk_ref[g]
+        wkv_ref[g, :, HD:] = wv_ref[g]
+        return 0
+
+    lax.fori_loop(0, wkv_ref.shape[0], merge, 0)
     next(sums[one])
     next(sums[two])
-    loads[2].wait()
-    loads[3].wait()
-    next(sums[one])
-    for step in RS_ORDER:
+    for step in (2, 1):
         spread(one, step)
+    next(sums[two])
     next(sums[three])
     next(sums[four])
-    next(sums[two])
     y_send(one)
+    for step in (-1, 0):
+        spread(one, step)
     copies["back", 3].wait_recv()
     copies["relayed", 0].wait_recv()
     copies["relayed", 1].wait_recv()
-    for g in range(4):
+    for g in range(0, 4):
         project(g, 1)
     next(sums[two])
+    next(sums[three])
     y_pass(one, 1)
     y_pass(one, -1)
-    next(sums[two])
-    next(sums[three])
     for step in RS_ORDER:
         spread(two, step)
+    next(sums[four])
+    next(sums[three])
+    y_send(two)
     for g in range(4, 8):
         project(g, 1)
     next(sums[three])
     next(sums[four])
-    y_send(two)
-    next(sums[three])
-    next(sums[four])
     y_pass(two, 1)
     y_pass(two, -1)
-    next(sums[three])
     for step in RS_ORDER:
         spread(three, step)
     next(sums[four])
     y_send(three)
     next(sums[four])
-    next(sums[four])
     for step in RS_ORDER:
         spread(four, step)
+    y_end(one)
     y_pass(three, 1)
     y_pass(three, -1)
     y_send(four)
-    y_end(one)
     y_end(two)
     y_pass(four, 1)
     y_pass(four, -1)
@@ -672,10 +698,12 @@
         in_specs=[anywhere] * 5,
         out_specs=vmem,
         scratch_shapes=[
+            pltpu.VMEM(terms.shape, bf),
             pltpu.VMEM(query_grad.shape, bf),
             pltpu.VMEM((2, size, query_grad.shape[1]), bf),
-            pltpu.VMEM(terms.shape, bf),
             pltpu.VMEM((blocks, columns, w_query.shape[1]), bf),
+            pltpu.VMEM((blocks, columns, HD), bf),
+            pltpu.VMEM((blocks, columns, HD), bf),
             pltpu.VMEM((blocks, columns, 2 * HD), bf),
             pltpu.VMEM((blocks, rows, columns), jnp.float32),
             pltpu.VMEM((rows, 2 * HD), bf),

time: 180 us -> 158 us (0.88)
  Pallas kernels: 176 us -> 155 us
    pallas_call x1, Pallas kernels: 57.4 us -> 44.9 us  [collect(): pl.pallas_call(collect_kernel, out_shape=[jax.ShapeDtypeStruct((SIDE * SI...]
    pallas_call x1, Pallas kernels: 35.2 us -> 30 us  [attention(): pl.pallas_call(functools.partial(attention_kernel, total), out_shape=[jax...]
    pallas_call x1, Pallas kernels: 83.4 us -> 80.1 us  [finish(): pl.pallas_call(finish_kernel, out_shape=jax.ShapeDtypeStruct((rows, colum...]
where the time goes in v4:
time: 158 us
  Pallas kernels  155 us (98%)
  local copies, waits for them, and re-layouts  1.98 us (1%)
    pallas_call x1, Pallas kernels, finish(): pl.pallas_call(finish_kernel, out_shape=jax.ShapeDtypeStruct((rows, colum...  80.1 us
    pallas_call x1, Pallas kernels, collect(): pl.pallas_call(collect_kernel, out_shape=[jax.ShapeDtypeStruct((SIDE * SI...  44.9 us
    pallas_call x1, Pallas kernels, attention(): pl.pallas_call(functools.partial(attention_kernel, total), out_shape=[jax...  30 us

profile of v4, /device:TPU:0, one launch (start us, length us, event | category | flops | bytes accessed | tf_op | source)
XLA Modules:
  0.0 157.7 jit_solution(12271095019999433895)
XLA Ops:
  0.0 0.6 pad_add_fusion.start_ref
  0.6 44.9 %collect.1 = (bf16[16,512,256]{2,1,0:T(8,128)(2,1)}, bf16[512,1024]{1,0:T(8,128)(2,1)}, bf16[512,1024]{1,0:T(8,128)(2,1)}, f32[16,512]{1,0:T(8,128)}) custom-call(bf16[512,128]{1,0:T(8,128)(2,1)} %k_ref.1, bf16[512,128]{1,0:T(8,128)(2,1)} %v_ref.1, bf16[512,1024]{1,0:T(8,128)(2,1)} %q_ref.1, bf16[512,1024]{1,0:T(8,128)(2,1)} %out_grad_ref.1, ...), custom_call_target="tpu_custom_call" | custom-call | tf_op jit(solution)/shard_map/collect/pallas_call | solution.py:414
  45.5 30.0 %attention.1 = (bf16[512,1024]{1,0:T(8,128)(2,1)}, bf16[8192,256]{1,0:T(8,128)(2,1)}) custom-call(s32[4]{0:T(128)} %pad_add_fusion.start_ref, s32[8]{0:T(128)} %lengths_ref.1, f32[16,512]{1,0:T(8,128)} %get-tuple-element.11.row_ref, bf16[512,1024]{1,0:T(8,128)(2,1)} %get-tuple-element.12.q_hbm, bf16[512,1024]{1,0:T(8,128)(2,1)} %get-tuple-element.13.do_hbm, ...), custom_call_target="tpu_custom_call" | custom-call | tf_op jit(solution)/shard_map/attention/pallas_call | solution.py:208
  75.6 80.1 %finish.1 = bf16[512,640]{1,0:T(8,128)(2,1)} custom-call(bf16[512,1024]{1,0:T(8,128)(2,1)} %get-tuple-element.15.dq_in, bf16[16,512,256]{2,1,0:T(8,128)(2,1)} %bitcast.11, bf16[8,640,1024]{2,1,0:T(8,128)(2,1)} %bitcast.9, bf16[8,640,128]{2,1,0:T(8,128)(2,1)} %bitcast.12, bf16[8,640,128]{2,1,0:T(8,128)(2,1)} %bitcast.13), custom_call_target="tpu_custom_call" | custom-call | tf_op jit(solution)/shard_map/finish/pallas_call | solution.py:695
  155.7 2.0 %copy.11 = bf16[512,640]{1,0:T(8,128)(2,1)} copy(bf16[512,640]{1,0:T(8,128)(2,1)} %finish.1) | data formatting | bytes 1310720

commit v5 on v4

--- a/solution.py
+++ b/solution.py
@@ -11,183 +11,190 @@
 NEG = -1e30
 SAFE = 60.0
 LAST = (((1,), (1,)), ((), ()))
-
-
 PIECES = 4
 
 
-def attention_kernel(total, start_ref, lengths_ref, row_ref, q_hbm, do_hbm, kv_hbm,
-                     dq_hbm, dkv_hbm, q_ref, do_ref, kv_ref, dq_ref, dkv_ref, load_sem, store_sem, e_ref, ds_ref, mt_ref, q_rows, do_rows, q_over, do_over, kt_ref, dqt_ref,
-                     dk_acc, dv_acc, stat_ref):
+def attention_kernel(total, start_ref, lengths_ref, row_ref, q_hbm, do_hbm, kv_hbm, dq_hbm, dkv_hbm,
+                     q_ref, do_ref, kv_ref, dq_ref, dkv_ref, load_sem, store_sem, e_ref, ds_ref, ds_other, q_rows, do_rows,
+                     q_turned, do_turned, delta_ref, top_ref, sum_ref, dq_acc, dk_acc, dv_acc):
     rows = q_rows.shape[0]
     heads = rows // CHUNK
     pair = 2 * CHUNK
     pairs = rows // pair
     chunks = q_ref.shape[0] // CHUNK
-    tiles = total // TILE
+    blocks = total // HD
     scale = HD ** -0.5
     to_log2 = scale * 1.4426950408889634
-
     piece = total // PIECES
-    loads = [pltpu.make_async_copy(kv_hbm.at[pl.ds(n * piece, piece), :], kv_ref.at[pl.ds(n * piece, piece), :],
-                                   load_sem.at[n]) for n in range(PIECES)]
+    loads = [pltpu.make_async_copy(kv_hbm.at[pl.ds(n * piece, piece), :],
+                                   kv_ref.at[pl.ds(CHUNK + n * piece, piece), :], load_sem.at[n])
+             for n in range(PIECES)]
     loads += [pltpu.make_async_copy(q_hbm, q_ref, load_sem.at[PIECES]),
               pltpu.make_async_copy(do_hbm, do_ref, load_sem.at[PIECES + 1])]
     for copy in loads:
         copy.start()
+    kv_ref[:CHUNK, :] = jnp.zeros((CHUNK, 2 * HD), jnp.bfloat16)
 
     def clear(i, _):
-        at = pl.ds(pl.multiple_of(i * TILE, TILE), TILE)
-        dk_acc[at, :] = jnp.zeros((TILE, HD), jnp.float32)
-        dv_acc[at, :] = jnp.zeros((TILE, HD), jnp.float32)
+        dk_acc[i] = jnp.zeros((HD, HD), jnp.float32)
+        dv_acc[i] = jnp.zeros((HD, HD), jnp.float32)
         return 0
 
-    lax.fori_loop(0, tiles, clear, 0)
-
-    def turn_keys(i, most):
-        turned = kv_ref[pl.ds(pl.multiple_of(i * TILE, TILE), TILE), :HD].T
-        kt_ref[i] = turned
-        wide = turned.astype(jnp.float32)
-        return jnp.maximum(most, jnp.sum(wide * wide, axis=0, keepdims=True))
-
-    key_most = jnp.zeros((1, TILE), jnp.float32)
+    lax.fori_loop(0, blocks + 1, clear, 0)
+
+    def measure_keys(i, most):
+        wide = kv_ref[pl.ds(pl.multiple_of(CHUNK + i * TILE, CHUNK), TILE), :HD].astype(jnp.float32)
+        return jnp.maximum(most, jnp.sum(wide * wide, axis=1, keepdims=True))
+
+    key_most = jnp.zeros((TILE, 1), jnp.float32)
     for n in range(PIECES):
         loads[n].wait()
-        key_most = lax.fori_loop(n * tiles // PIECES, (n + 1) * tiles // PIECES, turn_keys, key_most, unroll=4)
+        key_most = lax.fori_loop(n * piece // TILE, (n + 1) * piece // TILE, measure_keys, key_most)
     key_most = jnp.max(key_most)
     for copy in loads[PIECES:]:
         copy.wait()
 
     def one_chunk(j, _):
         first = start_ref[j]
+        end = first + CHUNK
         t0 = pl.multiple_of(j * CHUNK, CHUNK)
         for h in range(heads):
-            part = q_ref[pl.ds(t0, CHUNK), h * HD:(h + 1) * HD]
-            q_rows[h * CHUNK:(h + 1) * CHUNK, :] = part
-            do_rows[h * CHUNK:(h + 1) * CHUNK, :] = do_ref[pl.ds(t0, CHUNK), h * HD:(h + 1) * HD]
+            part = slice(h * CHUNK, (h + 1) * CHUNK)
+            q_rows[part, :] = q_ref[pl.ds(t0, CHUNK), h * HD:(h + 1) * HD]
+            do_rows[part, :] = do_ref[pl.ds(t0, CHUNK), h * HD:(h + 1) * HD]
+            delta_ref[part, :] = jnp.broadcast_to(row_ref[h:h + 1, pl.ds(t0, CHUNK)], (HD, CHUNK)).T
         small = jnp.max(row_ref[heads:, pl.ds(t0, CHUNK)]) * key_most * (to_log2 * to_log2) <= SAFE * SAFE
-        query_pos = first + lax.broadcasted_iota(jnp.int32, (1, pair), 1) % CHUNK
-        row_start = jnp.zeros((1, pair), jnp.int32)
         low, high = jnp.int32(0), jnp.int32(0)
         begin = jnp.int32(0)
+        begins = []
         for d in range(lengths_ref.shape[0]):
-            row_start = jnp.where(query_pos >= begin, begin, row_start)
             low = jnp.where(first >= begin, begin, low)
-            high = jnp.where(first + CHUNK - 1 >= begin, begin, high)
+            high = jnp.where(end - 1 >= begin, begin, high)
+            begins.append(begin)
             begin = begin + lengths_ref[d]
-        tile_low = low // TILE
-        tile_end = (first + CHUNK - 1) // TILE + 1
-        plain_low = jnp.minimum((high + TILE - 1) // TILE, tile_end)
-        plain_end = jnp.maximum((first + 1) // TILE, plain_low)
-        edge = plain_low - tile_low
-        edges = edge + tile_end - plain_end
-
-        def edge_tile(n):
-            return jnp.where(n < edge, tile_low + n, plain_end + n - edge)
+        count = (end - low + TILE - 1) // TILE
+        plain_end = jnp.maximum((end - high) // TILE, 1)
+        edges = 1 + count - plain_end
+
+        def edge_tile(m):
+            return jnp.where(m == 0, 0, plain_end + m - 1)
 
         def allowed_of(key0):
-            key_pos = key0 + lax.broadcasted_iota(jnp.int32, (TILE, pair), 0)
+            query_pos = first + lax.broadcasted_iota(jnp.int32, (CHUNK, TILE), 0)
+            key_pos = key0 + lax.broadcasted_iota(jnp.int32, (CHUNK, TILE), 1)
+            row_start = jnp.zeros((CHUNK, TILE), jnp.int32)
+            for one in begins:
+                row_start = jnp.where(query_pos >= one, one, row_start)
             return (key_pos >= row_start) & (key_pos <= query_pos)
 
+        def tile_at(n):
+            return pl.multiple_of(end - TILE * (n + 1) + CHUNK, CHUNK)
+
         def scores(key, p):
-            return lax.dot_general(key, q_rows[p * pair:(p + 1) * pair, :], LAST,
+            return lax.dot_general(q_rows[p * pair:(p + 1) * pair, :], key, LAST,
                                    preferred_element_type=jnp.float32) * to_log2
 
-        def weigh(i, sums, masked):
-            key0 = pl.multiple_of(i * TILE, TILE)
-            key = kv_ref[pl.ds(key0, TILE), :HD]
-            new = []
+        def hide(values, allowed, other):
+            return jnp.concatenate([jnp.where(allowed, values[:CHUNK], other),
+                                    jnp.where(allowed, values[CHUNK:], other)], axis=0)
+
+        def find_top(n, _):
+            key = kv_ref[pl.ds(tile_at(n), TILE), :HD]
+            allowed = allowed_of(tile_at(n) - CHUNK)
             for p in range(pairs):
-                e = jnp.exp2(scores(key, p))
-                if masked:
-                    e = jnp.where(allowed_of(key0), e, 0.0)
-                new.append(sums[p] + jnp.sum(e.reshape(TILE // 8, 8, pair), axis=0))
-                e_ref[i - tile_low, :, p * pair:(p + 1) * pair] = e.astype(jnp.bfloat16)
-            return tuple(new)
+                part = slice(p * pair, (p + 1) * pair)
+                s = hide(scores(key, p), allowed, NEG)
+                top_ref[part, :] = jnp.maximum(top_ref[part, :], jnp.maximum(s[:, :HD], s[:, HD:]))
+            return 0
+
+        def weigh(n, masked, shifted):
+            key = kv_ref[pl.ds(tile_at(n), TILE), :HD]
+            allowed = allowed_of(tile_at(n) - CHUNK) if masked else None
+            for p in range(pairs):
+                part = slice(p * pair, (p + 1) * pair)
+                s = scores(key, p)
+                if shifted:
+                    s = hide(s, allowed, NEG) - jnp.concatenate([top_ref[part, :], top_ref[part, :]], axis=1)
+                e = jnp.exp2(s)
+                if masked and not shifted:
+                    e = hide(e, allowed, 0.0)
+                sum_ref[part, :] += e[:, :HD] + e[:, HD:]
+                e_ref[n, part, :] = e.astype(jnp.bfloat16)
+            return 0
+
+        sum_ref[...] = jnp.zeros_like(sum_ref)
 
         @pl.when(small)
         def _():
-            sums = tuple(jnp.zeros((8, pair), jnp.float32) for _ in range(pairs))
-            sums = lax.fori_loop(0, edges, lambda n, s: weigh(edge_tile(n), s, True), sums)
-            sums = lax.fori_loop(plain_low, plain_end, lambda i, s: weigh(i, s, False), sums)
-            for p in range(pairs):
-                stat_ref[:, p * pair:(p + 1) * pair] = 1.0 / jnp.sum(sums[p], axis=0, keepdims=True)
+            lax.fori_loop(0, edges, lambda m, _: weigh(edge_tile(m), True, False), 0)
+            twos = (plain_end - 1) // 2
+
+            def two(m, _):
+                weigh(1 + 2 * m, False, False)
+                return weigh(2 + 2 * m, False, False)
+
+            lax.fori_loop(0, twos, two, 0)
+            lax.fori_loop(1 + 2 * twos, plain_end, lambda n, _: weigh(n, False, False), 0)
 
         @pl.when(jnp.logical_not(small))
         def _():
-            def step(i, carry):
-                tops, sums = carry
-                key0 = pl.multiple_of(i * TILE, TILE)
-                key = kv_ref[pl.ds(key0, TILE), :HD]
-                new_tops, new_sums = [], []
-                for p in range(pairs):
-                    s = jnp.where(allowed_of(key0), scores(key, p), NEG)
-                    top = jnp.maximum(tops[p], jnp.max(s, axis=0, keepdims=True))
-                    e = jnp.exp2(s - top)
-                    new_sums.append(sums[p] * jnp.exp2(tops[p] - top) + jnp.sum(e, axis=0, keepdims=True))
-                    new_tops.append(top)
-                    e_ref[i - tile_low, :, p * pair:(p + 1) * pair] = e.astype(jnp.bfloat16)
-                    mt_ref[i - tile_low, :, p * pair:(p + 1) * pair] = top
-                return tuple(new_tops), tuple(new_sums)
-
-            tops, sums = lax.fori_loop(tile_low, tile_end, step, (
-                tuple(jnp.full((1, pair), NEG, jnp.float32) for _ in range(pairs)),
-                tuple(jnp.zeros((1, pair), jnp.float32) for _ in range(pairs))))
-
-            def settle(i, _):
-                for p in range(pairs):
-                    part = slice(p * pair, (p + 1) * pair)
-                    factor = jnp.exp2(mt_ref[i - tile_low, :, part] - tops[p])
-                    e_ref[i - tile_low, :, part] = (
-                        e_ref[i - tile_low, :, part].astype(jnp.float32) * factor).astype(jnp.bfloat16)
-                return 0
-
-            lax.fori_loop(tile_low, tile_end, settle, 0)
-            for p in range(pairs):
-                stat_ref[:, p * pair:(p + 1) * pair] = 1.0 / sums[p]
+            top_ref[...] = jnp.full_like(top_ref, NEG)
+            lax.fori_loop(0, count, find_top, 0)
+            top_ref[...] = jnp.broadcast_to(jnp.max(top_ref[...], axis=1, keepdims=True), top_ref.shape)
+            lax.fori_loop(0, count, lambda n, _: weigh(n, True, True), 0)
 
         for h in range(heads):
             part = slice(h * CHUNK, (h + 1) * CHUNK)
-            inverse = jnp.broadcast_to(stat_ref[:, part], (HD, CHUNK)).T
-            q_over[part, :] = (q_rows[part, :].astype(jnp.float32) * inverse).astype(jnp.bfloat16)
-            do_over[part, :] = (do_rows[part, :].astype(jnp.float32) * inverse).astype(jnp.bfloat16)
-        delta = [jnp.concatenate([row_ref[2 * p:2 * p + 1, pl.ds(t0, CHUNK)],
-                                  row_ref[2 * p + 1:2 * p + 2, pl.ds(t0, CHUNK)]], axis=1) for p in range(pairs)]
-        dqt_ref[...] = jnp.zeros_like(dqt_ref)
-
-        def grad_step(i, _):
-            key0 = pl.multiple_of(i * TILE, TILE)
-            slot = i - tile_low
-            value = kv_ref[pl.ds(key0, TILE), HD:]
-            key_t = kt_ref[i]
+            inverse = jnp.broadcast_to(1.0 / jnp.sum(sum_ref[part, :], axis=1, keepdims=True), (CHUNK, HD))
+            sum_ref[part, :] = inverse
+            q_turned[:, part] = (q_rows[part, :].astype(jnp.float32) * inverse).astype(jnp.bfloat16).T
+            do_turned[:, part] = (do_rows[part, :].astype(jnp.float32) * inverse).astype(jnp.bfloat16).T
+        dq_acc[...] = jnp.zeros_like(dq_acc)
+
+        def grad_step(n, ds_ref):
+            at = tile_at(n)
+            block = at // HD
+            key = kv_ref[pl.ds(at, TILE), :HD]
+            value = kv_ref[pl.ds(at, TILE), HD:]
             for p in range(pairs):
                 part = slice(p * pair, (p + 1) * pair)
-                dp = lax.dot_general(value, do_rows[part, :], LAST, preferred_element_type=jnp.float32)
-                ds_ref[:, part] = (e_ref[slot, :, part].astype(jnp.float32) * (dp - delta[p])).astype(jnp.bfloat16)
-            dv_acc[pl.ds(key0, TILE), :] += jnp.dot(e_ref[slot], do_over[...], preferred_element_type=jnp.float32)
-            dk_acc[pl.ds(key0, TILE), :] += jnp.dot(ds_ref[...], q_over[...], preferred_element_type=jnp.float32)
-            dqt_ref[...] += jnp.dot(key_t, ds_ref[...], preferred_element_type=jnp.float32)
+                dp = lax.dot_general(do_rows[part, :], value, LAST, preferred_element_type=jnp.float32)
+                delta = delta_ref[part, :]
+                ds_ref[part, :] = (e_ref[n, part, :].astype(jnp.float32)
+                                   * (dp - jnp.concatenate([delta, delta], axis=1))).astype(jnp.bfloat16)
+            dv = jnp.dot(do_turned[...], e_ref[n], preferred_element_type=jnp.float32)
+            dv_acc[block] += dv[:, :HD]
+            dv_acc[block + 1] += dv[:, HD:]
+            dq_acc[...] += jnp.dot(ds_ref[...], key, preferred_element_type=jnp.float32)
+            dk = jnp.dot(q_turned[...], ds_ref[...], preferred_element_type=jnp.float32)
+            dk_acc[block] += dk[:, :HD]
+            dk_acc[block + 1] += dk[:, HD:]
             return 0
 
-        lax.fori_loop(tile_low, tile_end, grad_step, 0)
+        def grad_two(m, _):
+            grad_step(2 * m, ds_ref)
+            return grad_step(2 * m + 1, ds_other)
+
+        lax.fori_loop(0, count // 2, grad_two, 0)
+        lax.fori_loop(count // 2 * 2, count, lambda n, _: grad_step(n, ds_ref), 0)
         for h in range(heads):
             part = slice(h * CHUNK, (h + 1) * CHUNK)
             dq_ref[pl.ds(t0, CHUNK), h * HD:(h + 1) * HD] = (
-                dqt_ref[:, part] * (stat_ref[:, part] * scale)).T.astype(jnp.bfloat16)
+                dq_acc[part, :] * (sum_ref[part, :] * scale)).astype(jnp.bfloat16)
         pltpu.make_async_copy(dq_ref.at[pl.ds(t0, CHUNK), :], dq_hbm.at[pl.ds(t0, CHUNK), :], store_sem.at[j]).start()
         return 0
 
     lax.fori_loop(0, chunks, one_chunk, 0)
 
     def write(i, _):
-        at = pl.ds(pl.multiple_of(i * TILE, TILE), TILE)
-        dkv_ref[at, :HD] = (dk_acc[at, :] * scale).astype(jnp.bfloat16)
-        dkv_ref[at, HD:] = dv_acc[at, :].astype(jnp.bfloat16)
+        at = pl.ds(pl.multiple_of(i * HD, HD), HD)
+        dkv_ref[at, :HD] = (dk_acc[i + 1] * scale).astype(jnp.bfloat16).T
+        dkv_ref[at, HD:] = dv_acc[i + 1].astype(jnp.bfloat16).T
         return 0
 
     stores = []
     for n in range(PIECES):
-        lax.fori_loop(n * tiles // PIECES, (n + 1) * tiles // PIECES, write, 0)
+        lax.fori_loop(n * piece // HD, (n + 1) * piece // HD, write, 0, unroll=4)
         stores.append(pltpu.make_async_copy(dkv_ref.at[pl.ds(n * piece, piece), :],
                                             dkv_hbm.at[pl.ds(n * piece, piece), :], store_sem.at[chunks + n]))
         stores[-1].start()
@@ -202,35 +209,36 @@
     total = kv.shape[0]
     rows = q.shape[1] // HD * CHUNK
     max_tiles = (longest + CHUNK) // TILE + 2
+    bf = jnp.bfloat16
     vmem = pl.BlockSpec(memory_space=pltpu.VMEM)
     smem = pl.BlockSpec(memory_space=pltpu.SMEM)
     anywhere = pl.BlockSpec(memory_space=pl.ANY)
     return pl.pallas_call(
         functools.partial(attention_kernel, total),
-        out_shape=[jax.ShapeDtypeStruct(q.shape, jnp.bfloat16),
-                   jax.ShapeDtypeStruct(kv.shape, jnp.bfloat16)],
+        out_shape=[jax.ShapeDtypeStruct(q.shape, bf), jax.ShapeDtypeStruct(kv.shape, bf)],
         in_specs=[smem, smem, vmem] + [anywhere] * 3,
         out_specs=[anywhere] * 2,
         scratch_shapes=[
-            pltpu.VMEM(q.shape, jnp.bfloat16),
-            pltpu.VMEM(q.shape, jnp.bfloat16),
-            pltpu.VMEM(kv.shape, jnp.bfloat16),
-            pltpu.VMEM(q.shape, jnp.bfloat16),
-            pltpu.VMEM(kv.shape, jnp.bfloat16),
+            pltpu.VMEM(q.shape, bf),
+            pltpu.VMEM(q.shape, bf),
+            pltpu.VMEM((total + CHUNK, 2 * HD), bf),
+            pltpu.VMEM(q.shape, bf),
+            pltpu.VMEM(kv.shape, bf),
             pltpu.SemaphoreType.DMA((PIECES + 2,)),
             pltpu.SemaphoreType.DMA((q.shape[0] // CHUNK + PIECES,)),
-            pltpu.VMEM((max_tiles, TILE, rows), jnp.bfloat16),
-            pltpu.VMEM((TILE, rows), jnp.bfloat16),
-            pltpu.VMEM((max_tiles, 1, rows), jnp.float32),
-            pltpu.VMEM((rows, HD), jnp.bfloat16),
-            pltpu.VMEM((rows, HD), jnp.bfloat16),
-            pltpu.VMEM((rows, HD), jnp.bfloat16),
-            pltpu.VMEM((rows, HD), jnp.bfloat16),
-            pltpu.VMEM((total // TILE, HD, TILE), jnp.bfloat16),
-            pltpu.VMEM((HD, rows), jnp.float32),
-            pltpu.VMEM((total, HD), jnp.float32),
-            pltpu.VMEM((total, HD), jnp.float32),
-            pltpu.VMEM((1, rows), jnp.float32),
+            pltpu.VMEM((max_tiles, rows, TILE), bf),
+            pltpu.VMEM((rows, TILE), bf),
+            pltpu.VMEM((rows, TILE), bf),
+            pltpu.VMEM((rows, HD), bf),
+            pltpu.VMEM((rows, HD), bf),
+            pltpu.VMEM((HD, rows), bf),
+            pltpu.VMEM((HD, rows), bf),
+            pltpu.VMEM((rows, HD), jnp.float32),
+            pltpu.VMEM((rows, HD), jnp.float32),
+            pltpu.VMEM((rows, HD), jnp.float32),
+            pltpu.VMEM((rows, HD), jnp.float32),
+            pltpu.VMEM((total // HD + 1, HD, HD), jnp.float32),
+            pltpu.VMEM((total // HD + 1, HD, HD), jnp.float32),
         ],
         compiler_params=pltpu.CompilerParams(vmem_limit_bytes=62 * 2**20),
         name="attention",

time: 158 us -> 161 us (1.019)
  Pallas kernels: 155 us -> 158 us
    pallas_call x1, Pallas kernels: 30 us -> 34.2 us  [attention(): pl.pallas_call(functools.partial(attention_kernel, total), out_shape=[jax...]
where the time goes in v5:
time: 161 us
  Pallas kernels  158 us (98%)
  local copies, waits for them, and re-layouts  1.98 us (1%)
    pallas_call x1, Pallas kernels, finish(): pl.pallas_call(finish_kernel, out_shape=jax.ShapeDtypeStruct((rows, colum...  79.1 us
    pallas_call x1, Pallas kernels, collect(): pl.pallas_call(collect_kernel, out_shape=[jax.ShapeDtypeStruct((SIDE * SI...  44.9 us
    pallas_call x1, Pallas kernels, attention(): pl.pallas_call(functools.partial(attention_kernel, total), out_shape=[jax...  34.2 us

profile of v5, /device:TPU:0, one launch (start us, length us, event | category | flops | bytes accessed | tf_op | source)
XLA Modules:
  0.0 160.9 jit_solution(5097788726748994589)
XLA Ops:
  0.0 0.6 pad_add_fusion.start_ref
  0.6 44.9 %collect.1 = (bf16[16,512,256]{2,1,0:T(8,128)(2,1)}, bf16[512,1024]{1,0:T(8,128)(2,1)}, bf16[512,1024]{1,0:T(8,128)(2,1)}, f32[16,512]{1,0:T(8,128)}) custom-call(bf16[512,128]{1,0:T(8,128)(2,1)} %k_ref.1, bf16[512,128]{1,0:T(8,128)(2,1)} %v_ref.1, bf16[512,1024]{1,0:T(8,128)(2,1)} %q_ref.1, bf16[512,1024]{1,0:T(8,128)(2,1)} %out_grad_ref.1, ...), custom_call_target="tpu_custom_call" | custom-call | tf_op jit(solution)/shard_map/collect/pallas_call | solution.py:422
  45.5 34.2 %attention.1 = (bf16[512,1024]{1,0:T(8,128)(2,1)}, bf16[8192,256]{1,0:T(8,128)(2,1)}) custom-call(s32[4]{0:T(128)} %pad_add_fusion.start_ref, s32[8]{0:T(128)} %lengths_ref.1, f32[16,512]{1,0:T(8,128)} %get-tuple-element.11.row_ref, bf16[512,1024]{1,0:T(8,128)(2,1)} %get-tuple-element.12.q_hbm, bf16[512,1024]{1,0:T(8,128)(2,1)} %get-tuple-element.13.do_hbm, ...), custom_call_target="tpu_custom_call" | custom-call | tf_op jit(solution)/shard_map/attention/pallas_call | solution.py:216
  79.8 79.1 %finish.1 = bf16[512,640]{1,0:T(8,128)(2,1)} custom-call(bf16[512,1024]{1,0:T(8,128)(2,1)} %get-tuple-element.15.dq_in, bf16[16,512,256]{2,1,0:T(8,128)(2,1)} %bitcast.11, bf16[8,640,1024]{2,1,0:T(8,128)(2,1)} %bitcast.9, bf16[8,640,128]{2,1,0:T(8,128)(2,1)} %bitcast.12, bf16[8,640,128]{2,1,0:T(8,128)(2,1)} %bitcast.13), custom_call_target="tpu_custom_call" | custom-call | tf_op jit(solution)/shard_map/finish/pallas_call | solution.py:703
  158.9 2.0 %copy.11 = bf16[512,640]{1,0:T(8,128)(2,1)} copy(bf16[512,640]{1,0:T(8,128)(2,1)} %finish.1) | data formatting | bytes 1310720

commit v6 on v5

--- a/solution.py
+++ b/solution.py
@@ -14,8 +14,8 @@
 PIECES = 4
 
 
-def attention_kernel(total, start_ref, lengths_ref, row_ref, q_hbm, do_hbm, kv_hbm, dq_hbm, dkv_hbm,
-                     q_ref, do_ref, kv_ref, dq_ref, dkv_ref, load_sem, store_sem, e_ref, ds_ref, ds_other, q_rows, do_rows,
+def attention_kernel(total, lengths_ref, row_ref, q_hbm, do_hbm, kv_hbm, dq_hbm, dkv_hbm,
+                     q_ref, do_ref, kv_ref, dq_ref, dkv_ref, load_sem, store_sem, e_ref, ds_ref, ds_other, ds_third, q_rows, do_rows,
                      q_turned, do_turned, delta_ref, top_ref, sum_ref, dq_acc, dk_acc, dv_acc):
     rows = q_rows.shape[0]
     heads = rows // CHUNK
@@ -55,7 +55,7 @@
         copy.wait()
 
     def one_chunk(j, _):
-        first = start_ref[j]
+        first = work_start(j, chunks * CHUNK)
         end = first + CHUNK
         t0 = pl.multiple_of(j * CHUNK, CHUNK)
         for h in range(heads):
@@ -127,14 +127,15 @@
         @pl.when(small)
         def _():
             lax.fori_loop(0, edges, lambda m, _: weigh(edge_tile(m), True, False), 0)
-            twos = (plain_end - 1) // 2
-
-            def two(m, _):
-                weigh(1 + 2 * m, False, False)
-                return weigh(2 + 2 * m, False, False)
-
-            lax.fori_loop(0, twos, two, 0)
-            lax.fori_loop(1 + 2 * twos, plain_end, lambda n, _: weigh(n, False, False), 0)
+            fours = (plain_end - 1) // 4
+
+            def four(m, _):
+                for u in range(4):
+                    weigh(1 + 4 * m + u, False, False)
+                return 0
+
+            lax.fori_loop(0, fours, four, 0)
+            lax.fori_loop(1 + 4 * fours, plain_end, lambda n, _: weigh(n, False, False), 0)
 
         @pl.when(jnp.logical_not(small))
         def _():
@@ -171,12 +172,13 @@
             dk_acc[block + 1] += dk[:, HD:]
             return 0
 
-        def grad_two(m, _):
-            grad_step(2 * m, ds_ref)
-            return grad_step(2 * m + 1, ds_other)
-
-        lax.fori_loop(0, count // 2, grad_two, 0)
-        lax.fori_loop(count // 2 * 2, count, lambda n, _: grad_step(n, ds_ref), 0)
+        def grad_three(m, _):
+            grad_step(3 * m, ds_ref)
+            grad_step(3 * m + 1, ds_other)
+            return grad_step(3 * m + 2, ds_third)
+
+        lax.fori_loop(0, count // 3, grad_three, 0)
+        lax.fori_loop(count // 3 * 3, count, lambda n, _: grad_step(n, ds_ref), 0)
         for h in range(heads):
             part = slice(h * CHUNK, (h + 1) * CHUNK)
             dq_ref[pl.ds(t0, CHUNK), h * HD:(h + 1) * HD] = (
@@ -205,7 +207,7 @@
         copy.wait()
 
 
-def attention(starts, lengths, q, do, row_info, kv, longest=4608):
+def attention(lengths, q, do, row_info, kv, longest=4608):
     total = kv.shape[0]
     rows = q.shape[1] // HD * CHUNK
     max_tiles = (longest + CHUNK) // TILE + 2
@@ -216,7 +218,7 @@
     return pl.pallas_call(
         functools.partial(attention_kernel, total),
         out_shape=[jax.ShapeDtypeStruct(q.shape, bf), jax.ShapeDtypeStruct(kv.shape, bf)],
-        in_specs=[smem, smem, vmem] + [anywhere] * 3,
+        in_specs=[smem, vmem] + [anywhere] * 3,
         out_specs=[anywhere] * 2,
         scratch_shapes=[
             pltpu.VMEM(q.shape, bf),
@@ -227,6 +229,7 @@
             pltpu.SemaphoreType.DMA((PIECES + 2,)),
             pltpu.SemaphoreType.DMA((q.shape[0] // CHUNK + PIECES,)),
             pltpu.VMEM((max_tiles, rows, TILE), bf),
+            pltpu.VMEM((rows, TILE), bf),
             pltpu.VMEM((rows, TILE), bf),
             pltpu.VMEM((rows, TILE), bf),
             pltpu.VMEM((rows, HD), bf),
@@ -242,7 +245,7 @@
         ],
         compiler_params=pltpu.CompilerParams(vmem_limit_bytes=62 * 2**20),
         name="attention",
-    )(starts, lengths, row_info, q, do, kv)
+    )(lengths, row_info, q, do, kv)
 
 
 SIDE = 4
@@ -387,12 +390,17 @@
         copies[h, "line", 3].wait_recv()
         near(h, 3, shifts[3])
         keep(block_at(0, 2, 0), h)
+    for item in (1, 2):
+        for h in (0, 1):
+            far(h, item, shifts[item])
+            keep(block_at(0, shifts[item], 1), h)
+            keep(block_at(0, shifts[item], -1), h)
     for n, (src, dst) in enumerate(pairs):
         for step, slot in RELAY:
             part = pl.ds(2 * quarter + slot * (quarter // 2), quarter // 2)
             copies["relay", n, slot].wait_recv()
             begin(("relayed", n, slot), 48 + 2 * n + slot, (0, step), relay.at[n, slot], dst.at[part, :])
-    for item in (1, 2, 3):
+    for item in (3,):
         for h in (0, 1):
             far(h, item, shifts[item])
             keep(block_at(0, shifts[item], 1), h)
@@ -483,18 +491,20 @@
     def ident(s, h, k):
         return (s * 2 + h) * 5 + (4 if k is None else RS_ORDER.index(k))
 
-    def term(s, h, k, shift, start, count):
+    def term(s, h, k, shift, start, count, source=dkv_ref):
         if k is None:
             return res_ref.at[s, h, RS_ORDER.index(shift), pl.ds(start, count), :]
-        return dkv_ref.at[block_at(FIRST_AXIS[s][h], k, shift), pl.ds(s * part_rows + h * size + start, count), :]
+        return source.at[block_at(FIRST_AXIS[s][h], k, shift), pl.ds(s * part_rows + h * size + start, count), :]
 
     def ring_axis(s, h, k):
         return FIRST_AXIS[s][h] if k is None else 1 - FIRST_AXIS[s][h]
 
     def reduce_send(s, h, k):
         n, axis = ident(s, h, k), ring_axis(s, h, k)
-        begin(("low", n), 4 * n, {"ctx": ring_place(axis, 1)}, term(s, h, k, 2, 0, mid), low_ref.at[n])
-        begin(("high", n), 4 * n + 1, {"ctx": ring_place(axis, -1)}, term(s, h, k, 2, mid, mid), high_ref.at[n])
+        begin(("low", n), 4 * n, {"ctx": ring_place(axis, 1)}, term(s, h, k, 2, 0, mid, dkv_hbm),
+              low_ref.at[n])
+        begin(("high", n), 4 * n + 1, {"ctx": ring_place(axis, -1)}, term(s, h, k, 2, mid, mid, dkv_hbm),
+              high_ref.at[n])
 
     def reduce_pass(s, h, k):
         n, axis = ident(s, h, k), ring_axis(s, h, k)
@@ -550,12 +560,12 @@
     back = 48 * PARTS
 
     def give_back():
+        for j, step in ((1, -1), (3, 1)):
+            part = pl.ds(j * part_rows, part_rows)
+            begin(("back", j), back + 2 + j // 2, {"ctx": ring_place(0, step)}, dq_in.at[part, :], dq_ref.at[part, :])
         for step, slot in RELAY:
             part = pl.ds(2 * part_rows + slot * size, size)
             begin(("relay", slot), back + slot, {"ctx": ring_place(0, step)}, dq_in.at[part, :], relay.at[slot])
-        for j, step in ((1, -1), (3, 1)):
-            part = pl.ds(j * part_rows, part_rows)
-            begin(("back", j), back + 2 + j // 2, {"ctx": ring_place(0, step)}, dq_in.at[part, :], dq_ref.at[part, :])
 
     def relay_back():
         for step, slot in RELAY:
@@ -609,26 +619,31 @@
 
     sums = {s: reduce_steps(s) for s in PART_ORDER}
     one, two, three, four = PART_ORDER
-    loads[0].wait()
     next(sums[one])
     next(sums[two])
     give_back()
+    next(sums[three])
+    loads[0].wait()
     next(sums[one])
-    next(sums[three])
+    next(sums[four])
     next(sums[two])
-    next(sums[one])
-    relay_back()
-    next(sums[one])
     loads[1].wait()
     loads[4].wait()
     copies["back", 1].wait_recv()
-    for g in range(0, 4):
+    for g in range(0, 2):
         project(g, 0)
     next(sums[one])
+    next(sums[three])
+    for g in range(2, 4):
+        project(g, 0)
+    next(sums[one])
+    relay_back()
     next(sums[two])
-    next(sums[three])
     next(sums[four])
-    for g in range(4, 8):
+    for g in range(4, 6):
+        project(g, 0)
+    next(sums[one])
+    for g in range(6, 8):
         project(g, 0)
     loads[2].wait()
     loads[3].wait()
@@ -641,45 +656,46 @@
     lax.fori_loop(0, wkv_ref.shape[0], merge, 0)
     next(sums[one])
     next(sums[two])
-    for step in (2, 1):
+    for step in RS_ORDER:
         spread(one, step)
+    y_send(one)
     next(sums[two])
     next(sums[three])
+    next(sums[two])
     next(sums[four])
-    y_send(one)
-    for step in (-1, 0):
-        spread(one, step)
     copies["back", 3].wait_recv()
     copies["relayed", 0].wait_recv()
     copies["relayed", 1].wait_recv()
-    for g in range(0, 4):
+    for g in range(0, 2):
         project(g, 1)
-    next(sums[two])
     next(sums[three])
     y_pass(one, 1)
     y_pass(one, -1)
+    for g in range(2, 4):
+        project(g, 1)
     for step in RS_ORDER:
         spread(two, step)
+    y_send(two)
+    next(sums[three])
     next(sums[four])
-    next(sums[three])
-    y_send(two)
-    for g in range(4, 8):
+    for g in range(4, 6):
         project(g, 1)
     next(sums[three])
     next(sums[four])
+    for g in range(6, 8):
+        project(g, 1)
     y_pass(two, 1)
     y_pass(two, -1)
     for step in RS_ORDER:
         spread(three, step)
-    next(sums[four])
     y_send(three)
     next(sums[four])
     for step in RS_ORDER:
         spread(four, step)
+    y_send(four)
     y_end(one)
     y_pass(three, 1)
     y_pass(three, -1)
-    y_send(four)
     y_end(two)
     y_pass(four, 1)
     y_pass(four, -1)
@@ -736,11 +752,14 @@
       w_value.reshape(blocks, columns, -1))
 
 
+def work_start(j, rows):
+    me = lax.axis_index("ctx")
+    x, z = me // SIDE, me % SIDE
+    return (lax.rem(x - j + SIDE, SIDE) * SIDE + z) * rows + j * CHUNK
+
 def shards(queries, keys, values, outputs, out_grad, lengths, w_query, w_key, w_value):
-    rows = queries.shape[0]
-    starts = jnp.stack([ring_place(0, -j) * rows + j * CHUNK for j in range(SIDE)]).astype(jnp.int32)
     collected, q_work, grad_work, row_info = collect(keys, values, queries, out_grad, outputs)
-    query_grad, terms = attention(starts, lengths, q_work, grad_work, row_info, collected.reshape(-1, 2 * HD))
+    query_grad, terms = attention(lengths, q_work, grad_work, row_info, collected.reshape(-1, 2 * HD))
     return finish(query_grad, terms.reshape(collected.shape), w_query, w_key, w_value)
 
 

time: 161 us -> 159 us (0.988)
    pallas_call x1, Pallas kernels: 79.1 us -> 59.4 us  [finish(): pl.pallas_call(finish_kernel, out_shape=jax.ShapeDtypeStruct((rows, colum...]
    pallas_call x1, Pallas kernels: 34.2 us -> 53.8 us  [attention(): pl.pallas_call(functools.partial(attention_kernel, total), out_shape=[jax...]
where the time goes in v6:
time: 159 us; the launch traced here: 160 us
  Pallas kernels  158 us (99%)
  local copies, waits for them, and re-layouts  1.98 us (1%)
    pallas_call x1, Pallas kernels, finish(): pl.pallas_call(finish_kernel, out_shape=jax.ShapeDtypeStruct((rows, colum...  59.4 us
    pallas_call x1, Pallas kernels, attention(): pl.pallas_call(functools.partial(attention_kernel, total), out_shape=[jax...  53.8 us
    pallas_call x1, Pallas kernels, collect(): pl.pallas_call(collect_kernel, out_shape=[jax.ShapeDtypeStruct((SIDE * SI...  44.9 us

profile of v6, /device:TPU:0, one launch (start us, length us, event | category | flops | bytes accessed | tf_op | source)
XLA Modules:
  0.0 160.2 jit_solution(3476841838978496491)
XLA Ops:
  0.0 44.9 %collect.1 = (bf16[16,512,256]{2,1,0:T(8,128)(2,1)}, bf16[512,1024]{1,0:T(8,128)(2,1)}, bf16[512,1024]{1,0:T(8,128)(2,1)}, f32[16,512]{1,0:T(8,128)}) custom-call(bf16[512,128]{1,0:T(8,128)(2,1)} %k_ref.1, bf16[512,128]{1,0:T(8,128)(2,1)} %v_ref.1, bf16[512,1024]{1,0:T(8,128)(2,1)} %q_ref.1, bf16[512,1024]{1,0:T(8,128)(2,1)} %out_grad_ref.1, ...), custom_call_target="tpu_custom_call" | custom-call | tf_op jit(solution)/shard_map/collect/pallas_call | solution.py:430
  44.9 53.8 %attention.1 = (bf16[512,1024]{1,0:T(8,128)(2,1)}, bf16[8192,256]{1,0:T(8,128)(2,1)}) custom-call(s32[8]{0:T(128)} %lengths_ref.1, f32[16,512]{1,0:T(8,128)} %get-tuple-element.11.row_ref, bf16[512,1024]{1,0:T(8,128)(2,1)} %get-tuple-element.12.q_hbm, bf16[512,1024]{1,0:T(8,128)(2,1)} %get-tuple-element.13.do_hbm, bf16[8192,256]{1,0:T(8,128)(2,1)} %bitcast.6), custom_call_target="tpu_custom_call" | custom-call | tf_op jit(solution)/shard_map/attention/pallas_call | solution.py:218
  98.7 59.4 %finish.1 = bf16[512,640]{1,0:T(8,128)(2,1)} custom-call(bf16[512,1024]{1,0:T(8,128)(2,1)} %get-tuple-element.15.dq_in, bf16[16,512,256]{2,1,0:T(8,128)(2,1)} %bitcast.7, bf16[8,640,1024]{2,1,0:T(8,128)(2,1)} %bitcast.5, bf16[8,640,128]{2,1,0:T(8,128)(2,1)} %bitcast.8, bf16[8,640,128]{2,1,0:T(8,128)(2,1)} %bitcast.9), custom_call_target="tpu_custom_call" | custom-call | tf_op jit(solution)/shard_map/finish/pallas_call | solution.py:719
  158.2 2.0 %copy.11 = bf16[512,640]{1,0:T(8,128)(2,1)} copy(bf16[512,640]{1,0:T(8,128)(2,1)} %finish.1) | data formatting | bytes 1310720
